TPU v7x, 128 devices: a whole 4x4x4 slice. The times are simulated.
128 devices in a mesh: clus: 4 (over x), split: 32 (over z, y, core).
Axes of the slice: x: 4, y: 4, z: 4, core: 2. Of those that a mesh axis runs over, the one named last changes fastest.
Arguments:
- embeddings: float32 [16384, 4096], P(('clus', 'split'))
- cluster_ids: int32 [16384], P(('clus', 'split')), may hold values from 0 to 63, as said below
Outputs:
- best_similarity: float32 [16384], P(('clus', 'split'))
Inputs may be any that keep to these rules, and one draw needn't show every extreme that they name: `cluster_ids`: the documents of one device's shard hold at most 64 cluster ids with any one residue modulo 4, and every shard has a residue reached exactly 64 times. Some clusters hold a single document.
All inputs are finite; a program needn't handle non-finite values.
Results may differ from a plain program's by a relative error of at most 0.0003.
Values may be sent and summed in bfloat16 or wider, within the bound.
No kernel may reach another device: no remote copies, remote signals or barrier semaphores. Data moves between devices by JAX's collectives and lax.ppermute only.
A program may use at most 192 MiB of HBM per device.

v0:
```python
import functools

import jax
import jax.numpy as jnp
from jax import lax
from jax.experimental import pallas as pl
from jax.experimental.pallas import tpu as pltpu
from jax.sharding import Mesh, PartitionSpec as P

ROWS = 128
HALF_WIDTH = 2048
WIDTH = 512
LABEL_ROWS = 16
BINS = 16
CHIPS = 64
TRIES = ((24, 11), (32, 16))
GROUP = 32
GUESTS = 64
GUEST = 4096
LANES = 128
CAPS = (704, 512, 320, 192)
STARTS = (0, 704, 1216, 1536)
UNIT = 32
SHARES = (
    ((0, 0), (0, 256), (2, 0), (2, 128), (2, 256), (3, 0)),
    ((0, 128), (0, 384), (0, 512), (0, 640), (1, 0), (1, 128), (1, 256), (1, 384), (3, 128)),
)
BASES = ({0: 0, 2: 704, 3: 1024}, {0: -128, 1: 576, 3: 960})
SHARE_ROWS = 1216
SEGMENTS = (
    (0, 128, 0, None), (128, 576, 128, 0), (704, 256, None, 576), (960, 256, None, 832),
    (1216, 320, 704, None), (1536, 128, 1024, None), (1664, 64, 1152, 1088),
)
f32, bf16, i32 = jnp.float32, jnp.bfloat16, jnp.int32
WHOLE = pl.BlockSpec(memory_space=pltpu.VMEM)


def params(mib):
    return pltpu.CompilerParams(vmem_limit_bytes=mib * 1024 * 1024)


def index_on(axis):
    return lax.axis_index(axis)


def iota(shape, dim):
    return lax.broadcasted_iota(i32, shape, dim)


def dot_last(a, b):
    return lax.dot_general(a, b, (((1,), (1,)), ((), ())), preferred_element_type=f32)


def dot(a, b):
    return lax.dot_general(a, b, (((1,), (0,)), ((), ())), preferred_element_type=f32)


def as_bf16(mask):
    return jnp.where(mask, 1.0, 0.0).astype(bf16)


def bin_of(labels):
    rank, residue = labels >> 2, labels & 3
    row, col = rank >> 2, rank & 3
    col = jnp.where((row & 1) == 1, 3 - col, col)
    return 4 * col + ((row - residue) & 3)


def label_rows(ids_ref):
    ids = jnp.concatenate([ids_ref[...].astype(f32), jnp.zeros((1, HALF_WIDTH - ROWS), f32)], axis=1)
    return jnp.broadcast_to(ids, (LABEL_ROWS, HALF_WIDTH)).astype(bf16)


def half_of(core):
    return pl.ds(pl.multiple_of(core * HALF_WIDTH, HALF_WIDTH), HALF_WIDTH)


def unit_send_kernel(x_ref, ids_ref, out_ref, scale_ref):
    x = x_ref[...]
    scale = lax.rsqrt(jnp.sum(x * x, axis=1, keepdims=True) + 1e-06)
    scale_ref[...] = jnp.broadcast_to(scale, scale_ref.shape)
    out_ref[:ROWS, :] = (x_ref[:, half_of(1 - index_on("c"))] * scale).astype(bf16)
    out_ref[ROWS:, :] = label_rows(ids_ref)


def unit_keep_kernel(x_ref, ids_ref, scale_ref, out_ref, half_ref, sem):
    copy = pltpu.make_async_copy(x_ref.at[:, half_of(index_on("c"))], half_ref, sem)
    copy.start()
    out_ref[ROWS:, :] = label_rows(ids_ref)
    copy.wait()
    out_ref[:ROWS, :] = (half_ref[...] * scale_ref[:, :1]).astype(bf16)


def passed_on(over, before):
    once = before(over, 1)
    twice = before(over, 2)
    return jnp.maximum(jnp.maximum(over, 0), jnp.maximum(over + once, over + once + twice))


def pack_kernel(block, keep_ref, got_ref, out_ref, code_ref):
    first = index_on("c") == 0
    kept = jnp.max(keep_ref[ROWS:, :ROWS].astype(f32), axis=0, keepdims=True)
    got = jnp.max(got_ref[ROWS:, :ROWS].astype(f32), axis=0, keepdims=True)
    labels = jnp.concatenate([jnp.where(first, kept, got), jnp.where(first, got, kept)], axis=0).astype(i32)
    bins = bin_of(labels)
    upper = as_bf16(iota((ROWS, ROWS), 0) < iota((ROWS, ROWS), 1))

    def ranks_within(masks):
        member = jnp.concatenate([jnp.where(mask, 1.0, 0.0) for mask in masks], axis=0)
        row, col = iota((member.shape[0],) * 2, 0), iota((member.shape[0],) * 2, 1)
        earlier = dot(as_bf16(((row >> 1) == (col >> 1)) & (col < row)), member.astype(bf16))
        ranks = member * (dot(member.astype(bf16), upper) + jnp.sum(earlier, axis=1, keepdims=True))
        rank = sum(ranks[2 * b:2 * b + 2] for b in range(len(masks)))
        return rank.astype(i32), jnp.sum(member, axis=1, keepdims=True)

    rank, sizes = ranks_within([bins == b for b in range(BINS)])
    quad, line = bins >> 2, bins & 3
    taken = []
    for at in range(4):
        size = jnp.zeros(labels.shape, f32)
        for b in range(at, BINS, 4):
            size = jnp.where(quad == b >> 2, sizes[2 * b:2 * b + 1] + sizes[2 * b + 1:2 * b + 2], size)
        taken.append(size.astype(i32) - (block - 1))
    stays = []
    for at in range(4):
        moved = passed_on(taken[at], lambda _, back: taken[(at - back) & 3])
        stays.append(taken[at] + (block - 1) - moved)

    def of_line(values, which):
        out = values[0]
        for at in range(1, 4):
            out = jnp.where(which == at, values[at], out)
        return out

    stay = of_line(stays, line)
    to_line = jnp.where(rank < stay, line, (line + 1) & 3)
    to_slot = jnp.where(rank < stay, rank, of_line(stays, to_line) + rank - stay)
    placed = to_slot < (block - 1)
    lane = jnp.where(placed, to_line * GROUP + to_slot, -1)
    place = jnp.where(placed, (quad * 4 + to_line) * block + to_slot, -1)
    code_ref[...] = jnp.concatenate([jnp.where(placed, bins * LANES + lane, -1)] * 4, axis=0)
    docs = 2 * ROWS
    flat = lambda v: jnp.concatenate([v[:1], v[1:]], axis=1)
    label_row = flat(labels)
    counts = dot_last(jnp.ones((8, docs), bf16), as_bf16(iota((LANES, docs), 0) == label_row))[:1]
    named = jnp.where(iota((8, docs), 0) == flat(quad), (label_row + 1).astype(f32), 0.0).astype(bf16)
    names = dot_last(named, as_bf16(iota((LANES, docs), 0) == flat(lane)))
    own = jnp.where(first, place[:1], place[1:])
    other = jnp.where(first, place[1:], place[:1])
    onehot = as_bf16(iota((BINS * block, docs), 0) == jnp.concatenate([own, other], axis=1))
    is_last = iota((block, WIDTH), 0) == (block - 1)
    for y in range(4):
        columns = slice(y * WIDTH, (y + 1) * WIDTH)
        x = jnp.concatenate([keep_ref[:ROWS, columns], got_ref[:ROWS, columns]], axis=0)
        packed = dot(onehot, x)
        for b in range(BINS):
            extra = jnp.concatenate([names[b // 4:b // 4 + 1], counts, jnp.zeros((1, 2 * LANES), f32)], axis=1)
            out_ref[4 * b + y] = jnp.where(is_last, extra, packed[b * block:(b + 1) * block]).astype(bf16)


def labels_of(block, x_ref):
    tail = x_ref[:, block - 8:, :2 * LANES].astype(f32)
    tail = jnp.max(jnp.where(iota(tail.shape, 1) == 7, tail, 0.0), axis=1)
    return tail[:, :LANES].astype(i32) - 1, tail[:, LANES:].astype(bf16)


def counts_of(chip_counts):
    row, col = iota((LANES, LANES), 0), iota((LANES, LANES), 1)
    in_bin = (bin_of(row) == col) & (row < 4 * BINS)
    counts = [dot(chip_counts, as_bf16(in_bin & ((row & 3) == r))) for r in range(4)]
    return counts, [jnp.sum(v, axis=0, keepdims=True) for v in counts]


def in_order(sizes):
    a, b = jnp.maximum(sizes[0], sizes[1]), jnp.minimum(sizes[0], sizes[1])
    c, d = jnp.maximum(sizes[2], sizes[3]), jnp.minimum(sizes[2], sizes[3])
    first, e = jnp.maximum(a, c), jnp.minimum(a, c)
    g, fourth = jnp.maximum(b, d), jnp.minimum(b, d)
    return first, jnp.maximum(e, g), jnp.minimum(e, g), fourth


def names_kernel(block, x_ref, guest_ref, line_ref, key_ref, pos_ref, meta_ref):
    z = index_on("z")
    labels, _ = labels_of(block, x_ref)
    row, col = iota((LANES, LANES), 0), iota((LANES, LANES), 1)
    lane = iota(labels.shape, 1)
    group = lane >> 5
    valid = labels >= 0
    home = bin_of(labels) & 3
    at_home = valid & (home == z)
    upper = as_bf16(row < col)
    lower = as_bf16(iota((CHIPS, CHIPS), 1) < iota((CHIPS, CHIPS), 0))
    members, n = [at_home & ((labels & 3) == r) for r in range(4)], []
    for member in members:
        size = jnp.sum(jnp.where(member, 1.0, 0.0), axis=0, keepdims=True)
        n.append(jnp.sum(size, axis=1, keepdims=True))
    wide = lambda v: jnp.broadcast_to(v, (1, LANES))
    meta_ref[...] = jnp.concatenate([wide(v) for v in in_order(n)] * 2, axis=0).astype(i32)
    pos = jnp.full(labels.shape, -1.0, f32)
    for r, member in enumerate(members):
        place = sum(
            jnp.where((n[q] > n[r]) | ((n[q] == n[r]) & (q < r)), 1.0, 0.0) for q in range(4) if q != r
        )
        start = jnp.where(
            place < 0.5, float(STARTS[0]),
            jnp.where(place < 1.5, float(STARTS[1]), jnp.where(place < 2.5, float(STARTS[2]), float(STARTS[3]))),
        )
        member16 = as_bf16(member)
        rank = dot(member16, upper) + jnp.sum(dot(lower, member16), axis=1, keepdims=True)
        pos = jnp.where(member, start + rank, pos)
    pos = pos.astype(i32)
    pos_ref[...] = pos
    guest = valid & (home != group)
    guest16 = as_bf16(guest)
    same = (row >> 5) == (col >> 5)
    turn = dot(guest16, as_bf16(same & (row < col))) + dot(dot(lower, guest16).astype(bf16), as_bf16(same))
    turn = turn.astype(i32)
    away = at_home & (group != z) & (turn < GUESTS)
    key_ref[...] = jnp.where(away, turn, -1)
    per, groups = 16, CHIPS // 16
    value = jnp.where(group == z, jnp.where(guest, GUEST + turn, pos + 1), 0).astype(f32)
    value = pltpu.roll(value, lax.rem(LANES - GROUP * z, LANES), 1)
    value = jnp.where(lane < block, value, 0.0)
    lined = jnp.zeros((8, per * block), f32)
    for t in range(per):
        rows = jnp.concatenate([value[per * g + t:per * g + t + 1] for g in range(groups)] * 2, axis=0)
        rows = jnp.concatenate([rows, jnp.zeros((8, per * block - LANES), f32)], axis=1)
        lined = lined + (pltpu.roll(rows, t * block, 1) if t else rows)
    slots = jnp.concatenate([lined[g:g + 1] for g in range(groups)], axis=1).astype(i32)
    line_ref[...] = jnp.broadcast_to(slots, line_ref.shape)
    onehot = as_bf16(iota((GUESTS, CHIPS * block), 0) + GUEST == slots)
    guest_ref[...] = dot(onehot, x_ref[...].reshape(CHIPS * block, WIDTH)).astype(bf16)


def sorted_rows(segment, slots, x):
    onehot = as_bf16(iota((segment[1], x.shape[0]), 0) + (segment[0] + 1) == slots)
    return dot(onehot, x).astype(bf16)


def sort_kernel(block, x_ref, line_ref, send_ref, mine_ref):
    x = x_ref[...].reshape(CHIPS * block, WIDTH)
    slots = line_ref[:1, :]
    for core in range(2):
        @pl.when(index_on("c") == core)
        def _():
            for segment in SEGMENTS:
                rows = sorted_rows(segment, slots, x)
                for out_ref, at in ((mine_ref, segment[2 + core]), (send_ref, segment[2 + 1 - core])):
                    if at is not None:
                        out_ref[at:at + segment[1], :] = rows


def fit_kernel(block, units, x_ref, meta_ref, over_ref, table_ref):
    _, chip_counts = labels_of(block, x_ref)
    counts, sizes = counts_of(chip_counts)
    ordered = in_order(sizes)
    over = jnp.zeros((1, LANES), f32)
    for size, cap in zip(ordered, CAPS):
        over = jnp.maximum(over, jnp.where(size > cap, 1.0, 0.0))
    for share in SHARES:
        length = 0.0
        for q, first in share:
            rows = jnp.maximum(jnp.floor((ordered[q] + (UNIT - 1.0)) * (1 / UNIT)) - first // UNIT, 0.0)
            length = length + jnp.where(rows >= 3.0, rows - 1.0, rows)
        over = jnp.maximum(over, jnp.where(length > 4 * units, 1.0, 0.0))
    taken = counts[0] + counts[1] + counts[2] + counts[3]
    lane = iota(taken.shape, 1) & 3
    before = lambda v, back: jnp.where(lane >= back, pltpu.roll(v, back, 1), pltpu.roll(v, LANES - 4 + back, 1))
    extra = taken - (block - 1)
    moved = passed_on(extra, before)
    held = jnp.sum(moved, axis=0, keepdims=True)
    over = jnp.maximum(over, jnp.where(held > GUESTS, 1.0, 0.0))
    full = extra + before(extra, 1) + before(extra, 2) + before(extra, 3) > 0
    full = jnp.where(full | (moved > block - 1), 1.0, 0.0)
    over = jnp.maximum(over, jnp.max(full, axis=0, keepdims=True))
    over_ref[...] = jnp.broadcast_to(jnp.max(over, axis=1, keepdims=True), over_ref.shape).astype(i32)
    y, c = index_on("y"), index_on("c")
    blocks, sizes = [], [size_of(meta_ref, q) for q in range(4)]
    for core, share in enumerate(SHARES):
        at = jnp.zeros((), i32)
        for q, first in share:
            length = length_of(sizes[q], first)
            blocks.append((jnp.where((c == core) & (length > 0), at, 4 * units), FIRST_ROW[q] + first // LANES, at))
            at = at + length
    for t in range(units):
        index = y * units + t
        col, start = jnp.asarray(15, i32), jnp.asarray(0, i32)
        for block_start, block_col, block_at in blocks:
            inside = index >= block_start
            col, start = jnp.where(inside, block_col, col), jnp.where(inside, block_at, start)
        turn = index - start
        unit = 4 * col + jnp.where(turn == 0, 2, jnp.where(turn == 1, 1, turn + 1))
        beside = jnp.where(turn == 0, 3 * UNIT, LANES)
        for entry, value in enumerate((unit >> 2, (unit & 3) * UNIT, beside, col)):
            table_ref[4 * t + entry:4 * t + entry + 1, :] = jnp.full((1, LANES), value, i32)


def add_guests(core, base_ref, guest_ref, far_ref, out_ref):
    guests, far = guest_ref[...], far_ref[:1, :]
    for segment in SEGMENTS:
        at, rows = segment[2 + core], segment[1]
        if at is not None:
            out_ref[at:at + rows, :] = base_ref[at:at + rows, :] + sorted_rows(segment, far, guests)


def blocks_of(core):
    for q, first in SHARES[core]:
        at = BASES[core][q] + first
        yield q, first, pl.ds(at, CAPS[q] - first), pl.ds(at, LANES)


RAW_ROWS = max(sum(CAPS[q] - first for q, first in share) for share in SHARES)


def own_kernel(x_ref, guest_ref, key_ref, pos_ref, raw_ref, far_ref, rows_ref):
    total = jnp.zeros((8, GUESTS), f32)
    step = 16
    for first in range(0, CHIPS, step):
        flat = lambda ref: jnp.concatenate([ref[s:s + 1, :] for s in range(first, first + step)], axis=1)
        places = flat(pos_ref) + 1
        parts = jnp.where(iota((8, step * LANES), 0) == 0, places >> 5, places & 31).astype(f32).astype(bf16)
        total = total + dot_last(parts, as_bf16(iota((GUESTS, step * LANES), 0) == flat(key_ref)))
    far_ref[...] = jnp.broadcast_to((32.0 * total[:1] + total[1:2]).astype(i32), far_ref.shape)
    for core in range(2):
        @pl.when(index_on("c") == core)
        def _():
            add_guests(core, x_ref, guest_ref, far_ref, rows_ref)
            at = 0
            for q, first, left, right in blocks_of(core):
                rows = CAPS[q] - first
                raw_ref[at:at + rows, :] = dot_last(rows_ref[left, :], rows_ref[right, :])
                at += rows


def size_of(meta_ref, q):
    return jnp.max(meta_ref[q:q + 1, :].astype(f32)).astype(i32)


def length_of(size, first):
    units = jnp.maximum(((size + UNIT - 1) >> 5) - first // UNIT, 0)
    return jnp.where(units >= 3, units - 1, units)


def folded(score):
    away = jnp.full((UNIT, LANES), -4.0, f32) if score.shape[0] < LANES else score[2 * UNIT:3 * UNIT]
    both = jnp.where(iota(away.shape, 1) < 3 * UNIT, away, pltpu.roll(score[:UNIT], 3 * UNIT, 1))
    rest = [score[3 * UNIT:]] if score.shape[0] > 3 * UNIT else []
    return jnp.concatenate([both, score[UNIT:2 * UNIT]] + rest, axis=0)


def gram_kernel(units, meta_ref, x_ref, guest_ref, far_ref, raw_ref, out0, out1, out2, out3, part_ref, rows_ref):
    y, c = index_on("y"), index_on("c")
    part_ref[...] = jnp.full(part_ref.shape, -4.0, f32)
    for core in range(2):
        @pl.when(c == core)
        def _():
            add_guests(core, x_ref, guest_ref, far_ref, rows_ref)
            at, to = 0, jnp.zeros((), i32)
            for q, first, left, right in blocks_of(core):
                rows = CAPS[q] - first
                score = raw_ref[at:at + rows, :] + dot_last(rows_ref[left, :], rows_ref[right, :])
                at += rows
                size = size_of(meta_ref, q)
                i, j = iota(score.shape, 0), iota(score.shape, 1)
                keep = (i < size - first) & (j < size - first) & (i != j)
                score = folded(jnp.where(keep, score, -4.0))
                part_ref[pl.ds(pl.multiple_of(to, UNIT), score.shape[0]), :] = score
                to = jnp.minimum(to + UNIT * length_of(size, first), 4 * units * UNIT)
    chunk = units * UNIT
    for shift, out in enumerate((out0, out1, out2, out3)):
        out[...] = part_ref[pl.ds(pl.multiple_of(lax.rem(y + shift, 4) * chunk, UNIT), chunk), :]


FIRST_ROW = (0, 6, 10, 13)


def max_kernel(units, table_ref, p0, p1, p2, p3, pos_ref, out_ref):
    best = jnp.full((16, LANES), -1.0, f32)
    sub, lane, row = iota((UNIT, LANES), 0), iota((UNIT, LANES), 1), iota((16, LANES), 0)
    for t in range(units):
        at = slice(t * UNIT, (t + 1) * UNIT)
        block = (p0[at, :] + p1[at, :]) + (p2[at, :] + p3[at, :])
        unit_row, offset, beside, col = (table_ref[4 * t + entry:4 * t + entry + 1, :] for entry in range(4))
        one, two = jnp.where(lane < beside, block, -4.0), jnp.where(lane < beside, -4.0, block)
        along = jnp.max(one, axis=1, keepdims=True)
        along = jnp.max(jnp.where(sub + offset == lane, along, -1.0), axis=0, keepdims=True)
        best = jnp.maximum(best, jnp.where(row == unit_row, along, -1.0))
        along = jnp.max(two, axis=1, keepdims=True)
        two = jnp.maximum(jnp.where(sub == lane, along, -1.0), pltpu.roll(two, UNIT, 1))
        down = jnp.max(jnp.maximum(one, two), axis=0, keepdims=True)
        best = jnp.maximum(best, jnp.where(row == col, down, -1.0))
    pos = pos_ref[...]
    pos = jnp.where(pos >= STARTS[1], pos + 64, pos)
    pos = jnp.where(pos >= STARTS[3] + 64, pos + 64, pos)
    row, lane = pos >> 7, pos & (LANES - 1)
    out = jnp.full(pos.shape, -1.0, f32)
    for r in range(15):
        value = jnp.broadcast_to(best[r:r + 1, :], pos.shape)
        value = jnp.take_along_axis(value, lane, axis=1, mode="promise_in_bounds")
        out = jnp.where(row == r, value, out)
    out_ref[:CHIPS, :] = out
    out_ref[CHIPS:, :] = out


def pick_kernel(v_ref, code_ref, out_ref):
    c = index_on("c")
    values = jnp.maximum(v_ref[:CHIPS, :], v_ref[CHIPS:, :])
    values = jnp.max(values.reshape(BINS, 4, LANES), axis=1)
    eye = iota((LANES, LANES), 0) == iota((LANES, LANES), 1)
    code = jnp.max(jnp.where(iota((8, ROWS), 0) == c, code_ref[...], -1), axis=0, keepdims=True)
    code = jnp.max(jnp.where(eye, code.astype(f32), -1.0), axis=1, keepdims=True).astype(i32)
    slot = iota((ROWS, LANES), 1)
    best = jnp.full((ROWS, LANES), -1.0, f32)
    for b in range(BINS):
        best = jnp.where(slot + b * LANES == code, values[b:b + 1], best)
    best = jnp.max(best, axis=1, keepdims=True)
    out_ref[...] = jnp.max(jnp.where(eye, best, -1.0), axis=0, keepdims=True)


def gather_groups(embeddings, cluster_ids):
    split = ("z", "y", "c")
    rows = embeddings.shape[0]
    groups = lax.axis_size("x")
    cap = 2 * rows // groups
    slots = groups * cap
    owner_of = cluster_ids % groups
    onehot = (owner_of[:, None] == jnp.arange(groups, dtype=i32)[None, :]).astype(i32)
    before = jnp.cumsum(onehot, axis=0) - onehot
    rank = jnp.sum(before * onehot, axis=1)
    place = owner_of * cap + rank
    picked = place[None, :] == jnp.arange(slots, dtype=i32)[:, None]
    filled = jnp.any(picked, axis=1)
    source = jnp.sum(jnp.where(picked, jnp.arange(rows, dtype=i32)[None, :], 0), axis=1)
    out_labels = jnp.where(filled, cluster_ids[source], -1)
    squares = jnp.sum(embeddings * embeddings, axis=1, keepdims=True)
    local_unit = (embeddings * lax.rsqrt(squares + 1e-06)).astype(bf16)
    outgoing_unit = jnp.where(filled[:, None], local_unit[source], jnp.zeros((), bf16))
    unit = lax.all_to_all(outgoing_unit, "x", split_axis=0, concat_axis=0, tiled=True)
    labels = lax.all_to_all(out_labels, "x", split_axis=0, concat_axis=0, tiled=True)
    members = lax.axis_size(split)

    def everywhere(v):
        copies = jnp.broadcast_to(v[None], (members,) + v.shape).reshape((members * slots,) + v.shape[1:])
        return lax.all_to_all(copies, split, split_axis=0, concat_axis=0, tiled=True)

    def add_slice(i, scores):
        part = lax.dynamic_slice_in_dim(unit, i * WIDTH, WIDTH, 1)
        return scores + dot_last(part, everywhere(part))

    scores = lax.fori_loop(0, embeddings.shape[1] // WIDTH, add_slice, jnp.zeros((slots, members * slots), f32))
    all_labels = everywhere(labels)
    own = lax.axis_index(split) * slots + jnp.arange(slots, dtype=i32)
    mask = (
        (labels[:, None] == all_labels[None, :])
        & (labels[:, None] >= 0)
        & (own[:, None] != jnp.arange(members * slots, dtype=i32)[None, :])
    )
    scores = jnp.where(mask, scores, -1.0)
    best = jnp.maximum(-1.0, jnp.max(scores, axis=1))
    returned = lax.all_to_all(best, "x", split_axis=0, concat_axis=0, tiled=True)
    return returned[place]


def route(block, units, embeddings, cluster_ids):
    shape = jax.ShapeDtypeStruct
    half = shape((ROWS + LABEL_ROWS, HALF_WIDTH), bf16)
    ids = cluster_ids.reshape(1, ROWS)
    send, scale = pl.pallas_call(
        unit_send_kernel, out_shape=(half, shape((ROWS, LANES), f32)),
        in_specs=[WHOLE, WHOLE], out_specs=(WHOLE, WHOLE), compiler_params=params(12), name="unit_send",
    )(embeddings, ids)
    got = lax.ppermute(send, "c", [(0, 1), (1, 0)])
    keep = pl.pallas_call(
        unit_keep_kernel, out_shape=half,
        in_specs=[pl.BlockSpec(memory_space=pl.ANY), WHOLE, WHOLE], out_specs=WHOLE,
        scratch_shapes=[pltpu.VMEM((ROWS, HALF_WIDTH), f32), pltpu.SemaphoreType.DMA],
        compiler_params=params(8), name="unit_keep",
    )(embeddings, ids, scale)
    packed, code = pl.pallas_call(
        functools.partial(pack_kernel, block),
        out_shape=(shape((CHIPS, block, WIDTH), bf16), shape((8, ROWS), i32)),
        in_specs=[WHOLE, WHOLE], out_specs=(WHOLE, WHOLE), compiler_params=params(20), name="pack",
    )(keep, got)
    packed = lax.all_to_all(packed, ("x", "z", "y"), 0, 0, tiled=True)
    table = shape((CHIPS, LANES), i32)
    guests, line, key, pos, meta = pl.pallas_call(
        functools.partial(names_kernel, block),
        out_shape=(shape((GUESTS, WIDTH), bf16), shape((8, CHIPS * block), i32), table, table, shape((8, LANES), i32)),
        in_specs=[WHOLE], out_specs=(WHOLE,) * 5, compiler_params=params(12), name="names",
    )(packed)
    brought = lax.ppermute(guests, "z", [(i, (i + 3) % 4) for i in range(4)])
    share = shape((SHARE_ROWS, WIDTH), bf16)
    send, mine = pl.pallas_call(
        functools.partial(sort_kernel, block), out_shape=(share, share),
        in_specs=[WHOLE] * 2, out_specs=(WHOLE,) * 2, compiler_params=params(24), name="sort",
    )(packed, line)
    brought, mine, send = lax.optimization_barrier((brought, mine, send))
    other = lax.ppermute(send, "c", [(0, 1), (1, 0)])
    swapped = lax.ppermute(brought, "c", [(0, 1), (1, 0)])
    raw, far = pl.pallas_call(
        own_kernel, out_shape=(shape((RAW_ROWS, LANES), f32), shape((8, GUESTS), i32)),
        in_specs=[WHOLE] * 4, out_specs=(WHOLE,) * 2,
        scratch_shapes=[pltpu.VMEM((SHARE_ROWS, WIDTH), bf16)],
        compiler_params=params(16), name="own",
        cost_estimate=pl.CostEstimate(flops=2 * RAW_ROWS * LANES * WIDTH, bytes_accessed=4 << 20, transcendentals=0),
    )(mine, brought, key, pos)
    partial = pl.pallas_call(
        functools.partial(gram_kernel, units),
        out_shape=[shape((units * UNIT, LANES), f32)] * 4,
        in_specs=[WHOLE] * 5, out_specs=[WHOLE] * 4,
        scratch_shapes=[pltpu.VMEM((4 * units * UNIT + CAPS[0], LANES), f32), pltpu.VMEM((SHARE_ROWS, WIDTH), bf16)],
        compiler_params=params(16), name="gram",
    )(meta, other, swapped, far, raw)
    arrived = [partial[0]] + [
        lax.ppermute(partial[s], "y", [(i, (i + s) % 4) for i in range(4)]) for s in (1, 2, 3)
    ]
    over, table = pl.pallas_call(
        functools.partial(fit_kernel, block, units),
        out_shape=(shape((8, LANES), i32), shape((4 * units, LANES), i32)),
        in_specs=[WHOLE, WHOLE], out_specs=(WHOLE, WHOLE), compiler_params=params(8), name="fit",
    )(packed, meta)
    arrived, fits, table = lax.optimization_barrier((arrived, over[0, 0] == 0, table))
    best = pl.pallas_call(
        functools.partial(max_kernel, units),
        out_shape=shape((2 * CHIPS, LANES), f32),
        in_specs=[WHOLE] * 6, out_specs=WHOLE, compiler_params=params(8), name="maxima",
    )(table, *arrived, pos)
    back = lax.all_to_all(best.reshape(2 * CHIPS, 1, LANES), ("c", "x", "z", "y"), 0, 0, tiled=True)
    back, fits = lax.optimization_barrier((back, fits))
    best = pl.pallas_call(
        pick_kernel,
        out_shape=shape((1, ROWS), f32),
        in_specs=[WHOLE, WHOLE], out_specs=WHOLE, compiler_params=params(8), name="pick",
    )(back.reshape(2 * CHIPS, LANES), code).reshape(ROWS)
    return best, fits


def on_device(embeddings, cluster_ids, tries=TRIES):
    if not tries:
        return gather_groups(embeddings, cluster_ids)
    best, fits = route(*tries[0], embeddings, cluster_ids)
    return lax.cond(
        fits,
        lambda best, embeddings, cluster_ids: best,
        lambda best, embeddings, cluster_ids: on_device(embeddings, cluster_ids, tries[1:]),
        best, embeddings, cluster_ids,
    )


def solution(mesh):
    axes = ("x", "z", "y", "c")
    grid = Mesh(mesh.devices.reshape(4, 4, 4, 2), axes)
    return jax.shard_map(
        on_device, mesh=grid, in_specs=(P(axes, None), P(axes)), out_specs=P(axes), check_vma=False
    )
```

profile of v0, /device:TPU:1, one launch (start us, length us, event | category | flops | bytes accessed | tf_op | source)
XLA Modules:
  0.0 82.6 jit_solution(8921945576135559089)
XLA Ops:
  0.0 0.0 copy-start.1
  0.0 0.0 copy-start
  0.0 2.0 %unit_send.3 = (bf16[144,2048]{1,0:T(8,128)(2,1)S(1)}, f32[128,128]{1,0:T(8,128)S(1)}) custom-call(f32[128,4096]{1,0:T(8,128)} %x_ref.3, s32[1,128]{1,0:T(1,128)} %bitcast.35), custom_call_target="tpu_custom_call" | custom-call | tf_op jit(solution)/shard_map/unit_send/pallas_call | solution.py:468
  2.0 1.5 %collective-permute-start.7 = (bf16[144,2048]{1,0:T(8,128)(2,1)S(1)}, bf16[144,2048]{1,0:T(8,128)(2,1)S(1)}, u32[]{:S(2)}, u32[]{:S(2)}) collective-permute-start(bf16[144,2048]{1,0:T(8,128)(2,1)S(1)} %get-tuple-element.154), channel_id=1, source_target_pairs={{0,1},{1,0},{2,3},{3,2},{4,5},{5,4},{6,7},{7,6},{8,9},{9,8},{10,11... | collective-permute-start | bytes 1769480 | tf_op jit(solution)/shard_map/ppermute | solution.py:472
  3.5 0.0 copy-done.1
  3.5 0.0 copy-done
  3.5 0.2 unit_keep.3.keep_ref
  3.7 1.4 %collective-permute-done.7.got_ref = bf16[144,2048]{1,0:T(8,128)(2,1)S(1)} collective-permute-done((bf16[144,2048]{1,0:T(8,128)(2,1)S(1)}, bf16[144,2048]{1,0:T(8,128)(2,1)S(1)}, u32[]{:S(2)}, u32[]{:S(2)}) %collective-permute-start.7) | collective-permute-done | bytes 589856 | tf_op jit(solution)/shard_map/ppermute | solution.py:472
  5.1 0.8 %pack.3 = (bf16[64,24,512]{2,1,0:T(8,128)(2,1)S(1)}, s32[8,128]{1,0:T(8,128)S(1)}) custom-call(bf16[144,2048]{1,0:T(8,128)(2,1)S(1)} %unit_keep.3.keep_ref, bf16[144,2048]{1,0:T(8,128)(2,1)S(1)} %collective-permute-done.7.got_ref), custom_call_target="tpu_custom_call" | custom-call | tf_op jit(solution)/shard_map/pack/pallas_call | solution.py:479
  6.0 33.4 %all_to_all.61.x_ref = bf16[64,24,512]{2,1,0:T(8,128)(2,1)S(1)} all-to-all(bf16[64,24,512]{2,1,0:T(8,128)(2,1)S(1)} %get-tuple-element.155), channel_id=1, replica_groups=mesh['x'=4,'z'=4,'y'=4,'c'=2] {'x','z','y'}, dimensions={0} | all-to-all | bytes 3145728 | tf_op jit(solution)/shard_map/all_to_all | solution.py:484
  39.4 1.5 %names.3 = (bf16[64,512]{1,0:T(8,128)(2,1)S(1)}, s32[8,1536]{1,0:T(8,128)S(1)}, s32[64,128]{1,0:T(8,128)S(1)}, s32[64,128]{1,0:T(8,128)S(1)}, s32[8,128]{1,0:T(8,128)S(1)}) custom-call(bf16[64,24,512]{2,1,0:T(8,128)(2,1)S(1)} %all_to_all.61.x_ref), custom_call_target="tpu_custom_call" | custom-call | tf_op jit(solution)/shard_map/names/pallas_call | solution.py:486
  40.9 0.1 collective-permute-start.8
  41.0 3.1 %sort.3 = (bf16[1216,512]{1,0:T(8,128)(2,1)S(1)}, bf16[1216,512]{1,0:T(8,128)(2,1)S(1)}) custom-call(bf16[64,24,512]{2,1,0:T(8,128)(2,1)S(1)} %all_to_all.61.x_ref, s32[8,1536]{1,0:T(8,128)S(1)} %get-tuple-element.158.line_ref), custom_call_target="tpu_custom_call" | custom-call | tf_op jit(solution)/shard_map/sort/pallas_call | solution.py:493
  44.1 0.0 collective-permute-done.8.guest_ref
  44.2 3.8 %collective-permute-start.9 = (bf16[1216,512]{1,0:T(8,128)(2,1)S(1)}, bf16[1216,512]{1,0:T(8,128)(2,1)S(1)}, u32[]{:S(2)}, u32[]{:S(2)}) collective-permute-start(bf16[1216,512]{1,0:T(8,128)(2,1)S(1)} %get-tuple-element.161), channel_id=1, source_target_pairs={{0,1},{1,0},{2,3},{3,2},{4,5},{5,4},{6,7},{7,6},{8,9},{9,8},{10,11... | collective-permute-start | bytes 3735560 | tf_op jit(solution)/shard_map/ppermute | solution.py:498
  48.0 0.0 collective-permute-start.10
  48.0 1.6 %own.3 = (f32[2496,128]{1,0:T(8,128)S(1)}, s32[8,64]{1,0:T(8,128)S(1)}) custom-call(bf16[1216,512]{1,0:T(8,128)(2,1)S(1)} %get-tuple-element.163.x_ref, bf16[64,512]{1,0:T(8,128)(2,1)S(1)} %collective-permute-done.8.guest_ref, s32[64,128]{1,0:T(8,128)S(1)} %get-tuple-element.164.key_ref, s32[64,128]{1,0:T(8,128)S(1)} %get-tuple-element.165.pos_ref), custom_call_target="tpu_custom_call" | custom-call | flops 327155712 | bytes 4194304 | tf_op jit(solution)/shard_map/own/pallas_call | solution.py:500
  49.5 1.1 %collective-permute-done.10.guest_ref = bf16[64,512]{1,0:T(8,128)(2,1)S(1)} collective-permute-done((bf16[64,512]{1,0:T(8,128)(2,1)S(1)}, bf16[64,512]{1,0:T(8,128)(2,1)S(1)}, u32[]{:S(2)}, u32[]{:S(2)}) %collective-permute-start.10) | collective-permute-done | bytes 65568 | tf_op jit(solution)/shard_map/ppermute | solution.py:499
  50.6 0.0 collective-permute-done.9.x_ref
  50.6 1.6 %gram.3 = (f32[352,128]{1,0:T(8,128)S(1)}, f32[352,128]{1,0:T(8,128)S(1)}, f32[352,128]{1,0:T(8,128)S(1)}, f32[352,128]{1,0:T(8,128)S(1)}) custom-call(s32[8,128]{1,0:T(8,128)S(1)} %get-tuple-element.156.meta_ref, bf16[1216,512]{1,0:T(8,128)(2,1)S(1)} %collective-permute-done.9.x_ref, bf16[64,512]{1,0:T(8,128)(2,1)S(1)} %collective-permute-done.10.guest_ref, ...), custom_call_target="tpu_custom_call" | custom-call | tf_op jit(solution)/shard_map/gram/pallas_call | solution.py:507
  52.3 0.4 collective-permute-start.11
  52.6 1.6 %collective-permute-start.12 = (f32[352,128]{1,0:T(8,128)S(1)}, f32[352,128]{1,0:T(8,128)S(1)}, u32[]{:S(2)}, u32[]{:S(2)}) collective-permute-start(f32[352,128]{1,0:T(8,128)S(1)} %get-tuple-element.170), channel_id=1, source_target_pairs={{0,4},{2,6},{4,0},{6,2},{1,5},{3,7},{5,1},{7,3},{8,12},{10,14},{12... | collective-permute-start | bytes 540680 | tf_op jit(solution)/shard_map/ppermute | solution.py:515
  54.2 1.2 %collective-permute-start.13 = (f32[352,128]{1,0:T(8,128)S(1)}, f32[352,128]{1,0:T(8,128)S(1)}, u32[]{:S(2)}, u32[]{:S(2)}) collective-permute-start(f32[352,128]{1,0:T(8,128)S(1)} %get-tuple-element.171), channel_id=1, source_target_pairs={{0,6},{2,0},{4,2},{6,4},{1,7},{3,1},{5,3},{7,5},{8,14},{10,8},{12,... | collective-permute-start | bytes 540680 | tf_op jit(solution)/shard_map/ppermute | solution.py:515
  55.5 0.6 fit.3
  56.1 0.5 slice.6
  57.2 6.2 %collective-permute-done.11.p1 = f32[352,128]{1,0:T(8,128)S(1)} collective-permute-done((f32[352,128]{1,0:T(8,128)S(1)}, f32[352,128]{1,0:T(8,128)S(1)}, u32[]{:S(2)}, u32[]{:S(2)}) %collective-permute-start.11) | collective-permute-done | bytes 180256 | tf_op jit(solution)/shard_map/ppermute | solution.py:515
  63.4 0.0 collective-permute-done.12.p2
  63.4 0.3 collective-permute-done.13.p3
  63.7 1.5 %maxima.3 = f32[128,128]{1,0:T(8,128)} custom-call(s32[44,128]{1,0:T(8,128)S(1)} %get-tuple-element.174.table_ref, f32[352,128]{1,0:T(8,128)S(1)} %get-tuple-element.175.p0, f32[352,128]{1,0:T(8,128)S(1)} %collective-permute-done.11.p1, f32[352,128]{1,0:T(8,128)S(1)} %collective-permute-done.12.p2, f32[352,128]{1,0:T(8,128)S(1)} %collective-permute-done.13.p3, ...), custom_call_target="tpu_custom_call" | custom-call | tf_op jit(solution)/shard_map/maxima/pallas_call | solution.py:523
  65.2 7.1 %all-to-all-start.8 = ((f32[128,1,128]{2,1,0:T(1,128)}), f32[128,1,128]{2,1,0:T(1,128)S(1)}, u32[]{:S(2)}, u32[]{:S(2)}) async-start(f32[128,1,128]{2,1,0:T(1,128)} %bitcast.17), calls=%async_computation.8 | async-start | bytes 131072 | tf_op jit(solution)/shard_map/all_to_all | solution.py:528
  72.3 9.5 %all-to-all-done.8 = f32[128,1,128]{2,1,0:T(1,128)S(1)} async-done(((f32[128,1,128]{2,1,0:T(1,128)}), f32[128,1,128]{2,1,0:T(1,128)S(1)}, u32[]{:S(2)}, u32[]{:S(2)}) %all-to-all-start.8) | async-done | bytes 65568 | tf_op jit(solution)/shard_map/all_to_all | solution.py:528
  81.8 0.8 pick.3
  (1 shorter events, 0.0 us)
Async XLA Ops:
  0.0 3.5 %copy-start.1 = (f32[128,4096]{1,0:T(8,128)S(1)}, f32[128,4096]{1,0:T(8,128)}, u32[]{:S(2)}) copy-start(f32[128,4096]{1,0:T(8,128)} %x_ref.3) | copy-start | bytes 6291460
  0.0 3.5 %copy-start = (s32[128]{0:T(128)S(1)}, s32[128]{0:T(128)}, u32[]{:S(2)}) copy-start(s32[128]{0:T(128)} %param.9) | copy-start | bytes 1540
  2.0 3.1 %collective-permute-start.7 = (bf16[144,2048]{1,0:T(8,128)(2,1)S(1)}, bf16[144,2048]{1,0:T(8,128)(2,1)S(1)}, u32[]{:S(2)}, u32[]{:S(2)}) collective-permute-start(bf16[144,2048]{1,0:T(8,128)(2,1)S(1)} %get-tuple-element.154), channel_id=1, source_target_pairs={{0,1},{1,0},{2,3},{3,2},{4,5},{5,4},{6,7},{7,6},{8,9},{9,8},{10,11... | collective-permute-start | bytes 1769480 | tf_op jit(solution)/shard_map/ppermute | solution.py:472
  40.9 3.2 %collective-permute-start.8 = (bf16[64,512]{1,0:T(8,128)(2,1)S(1)}, bf16[64,512]{1,0:T(8,128)(2,1)S(1)}, u32[]{:S(2)}, u32[]{:S(2)}) collective-permute-start(bf16[64,512]{1,0:T(8,128)(2,1)S(1)} %get-tuple-element.157), channel_id=1, source_target_pairs={{0,24},{8,0},{16,8},{24,16},{1,25},{9,1},{17,9},{25,17},{2,26},{10... | collective-permute-start | bytes 196616 | tf_op jit(solution)/shard_map/ppermute | solution.py:491
  44.2 6.5 %collective-permute-start.9 = (bf16[1216,512]{1,0:T(8,128)(2,1)S(1)}, bf16[1216,512]{1,0:T(8,128)(2,1)S(1)}, u32[]{:S(2)}, u32[]{:S(2)}) collective-permute-start(bf16[1216,512]{1,0:T(8,128)(2,1)S(1)} %get-tuple-element.161), channel_id=1, source_target_pairs={{0,1},{1,0},{2,3},{3,2},{4,5},{5,4},{6,7},{7,6},{8,9},{9,8},{10,11... | collective-permute-start | bytes 3735560 | tf_op jit(solution)/shard_map/ppermute | solution.py:498
  48.0 2.7 %collective-permute-start.10 = (bf16[64,512]{1,0:T(8,128)(2,1)S(1)}, bf16[64,512]{1,0:T(8,128)(2,1)S(1)}, u32[]{:S(2)}, u32[]{:S(2)}) collective-permute-start(bf16[64,512]{1,0:T(8,128)(2,1)S(1)} %collective-permute-done.8.guest_ref), channel_id=1, source_target_pairs={{0,1},{1,0},{2,3},{3,2},{4,5},{5,4},{6,7},{7,6},{8,9},{9,8},{10,11... | collective-permute-start | bytes 196616 | tf_op jit(solution)/shard_map/ppermute | solution.py:499
  52.3 11.1 %collective-permute-start.11 = (f32[352,128]{1,0:T(8,128)S(1)}, f32[352,128]{1,0:T(8,128)S(1)}, u32[]{:S(2)}, u32[]{:S(2)}) collective-permute-start(f32[352,128]{1,0:T(8,128)S(1)} %get-tuple-element.169), channel_id=1, source_target_pairs={{0,2},{2,4},{4,6},{6,0},{1,3},{3,5},{5,7},{7,1},{8,10},{10,12},{12... | collective-permute-start | bytes 540680 | tf_op jit(solution)/shard_map/ppermute | solution.py:515
  52.6 10.8 %collective-permute-start.12 = (f32[352,128]{1,0:T(8,128)S(1)}, f32[352,128]{1,0:T(8,128)S(1)}, u32[]{:S(2)}, u32[]{:S(2)}) collective-permute-start(f32[352,128]{1,0:T(8,128)S(1)} %get-tuple-element.170), channel_id=1, source_target_pairs={{0,4},{2,6},{4,0},{6,2},{1,5},{3,7},{5,1},{7,3},{8,12},{10,14},{12... | collective-permute-start | bytes 540680 | tf_op jit(solution)/shard_map/ppermute | solution.py:515
  54.2 9.5 %collective-permute-start.13 = (f32[352,128]{1,0:T(8,128)S(1)}, f32[352,128]{1,0:T(8,128)S(1)}, u32[]{:S(2)}, u32[]{:S(2)}) collective-permute-start(f32[352,128]{1,0:T(8,128)S(1)} %get-tuple-element.171), channel_id=1, source_target_pairs={{0,6},{2,0},{4,2},{6,4},{1,7},{3,1},{5,3},{7,5},{8,14},{10,8},{12,... | collective-permute-start | bytes 540680 | tf_op jit(solution)/shard_map/ppermute | solution.py:515
  65.2 16.6 %all-to-all-start.8 = ((f32[128,1,128]{2,1,0:T(1,128)}), f32[128,1,128]{2,1,0:T(1,128)S(1)}, u32[]{:S(2)}, u32[]{:S(2)}) async-start(f32[128,1,128]{2,1,0:T(1,128)} %bitcast.17), calls=%async_computation.8 | async-start | bytes 131072 | tf_op jit(solution)/shard_map/all_to_all | solution.py:528
where the time goes:
time: 82.8 us; the launch traced here: 82.6 us
  blocking collectives  33.4 us (40%)
  waiting for transfers between devices  18.4 us (22%)
  starting transfers between devices  15.7 us (19%)
  Pallas kernels  13.7 us (17%)
    all_to_all x1, blocking collectives, route(): packed = lax.all_to_all(packed, ('x', 'z', 'y'), 0, 0, tiled=True)  33.4 us
    all_to_all x1, waiting for transfers between devices, route(): lax.all_to_all(best.reshape(2 * CHIPS, 1, LANES), ('c', 'x', 'z', 'y'), 0...  9.47 us
    all_to_all x1, starting transfers between devices, route(): lax.all_to_all(best.reshape(2 * CHIPS, 1, LANES), ('c', 'x', 'z', 'y'), 0...  7.13 us
    ppermute x3, waiting for transfers between devices, route(): lax.ppermute(partial[s], 'y', [(i, (i + s) % 4) for i in range(4)])  6.47 us
    ppermute x1, starting transfers between devices, route(): other = lax.ppermute(send, 'c', [(0, 1), (1, 0)])  3.8 us
    ppermute x3, starting transfers between devices, route(): lax.ppermute(partial[s], 'y', [(i, (i + s) % 4) for i in range(4)])  3.22 us
    pallas_call x1, Pallas kernels, route(): pl.pallas_call(functools.partial(sort_kernel, block), out_shape=(share, s...  3.15 us
    pallas_call x1, Pallas kernels, route(): pl.pallas_call(unit_send_kernel, out_shape=(half, shape((ROWS, LANES), f3...  1.98 us
  transfers between devices with their start and end apart: 8, of which 5 were waited for; matrix products, arithmetic and copies ran while one was open for 1% of the time, Pallas kernels for 7%

commit v1 on v0

--- a/solution.py
+++ b/solution.py
@@ -512,7 +512,7 @@
         compiler_params=params(16), name="gram",
     )(meta, other, swapped, far, raw)
     arrived = [partial[0]] + [
-        lax.ppermute(partial[s], "y", [(i, (i + s) % 4) for i in range(4)]) for s in (1, 2, 3)
+        lax.ppermute(partial[s], "y", [(i, (i + s) % 4) for i in range(4)]) for s in (2, 3, 1)
     ]
     over, table = pl.pallas_call(
         functools.partial(fit_kernel, block, units),

time: 82.8 us -> 81.2 us (0.981)
  starting transfers between devices: 15.7 us -> 13.3 us
  waiting for transfers between devices: 18.4 us -> 19.3 us
    all_to_all x1, starting transfers between devices: 7.13 us -> 5.14 us  [route(): lax.all_to_all(best.reshape(2 * CHIPS, 1, LANES), ('c', 'x', 'z', 'y'), 0...]
    ppermute x3, waiting for transfers between devices: 6.47 us -> 7.35 us  [route(): lax.ppermute(partial[s], 'y', [(i, (i + s) % 4) for i in range(4)])]
  transfers between devices with their start and end apart: 8 -> 8, of which waited for: 5 -> 6; matrix products, arithmetic and copies ran while one was open for 1% -> 1% of each run, Pallas kernels for 7% -> 7%
where the time goes in v1:
time: 81.2 us; the launch traced here: 81 us
  blocking collectives  33.4 us (41%)
  waiting for transfers between devices  19.3 us (24%)
  Pallas kernels  13.7 us (17%)
  starting transfers between devices  13.3 us (16%)
    all_to_all x1, blocking collectives, route(): packed = lax.all_to_all(packed, ('x', 'z', 'y'), 0, 0, tiled=True)  33.4 us
    all_to_all x1, waiting for transfers between devices, route(): lax.all_to_all(best.reshape(2 * CHIPS, 1, LANES), ('c', 'x', 'z', 'y'), 0...  9.47 us
    ppermute x3, waiting for transfers between devices, route(): lax.ppermute(partial[s], 'y', [(i, (i + s) % 4) for i in range(4)])  7.35 us
    all_to_all x1, starting transfers between devices, route(): lax.all_to_all(best.reshape(2 * CHIPS, 1, LANES), ('c', 'x', 'z', 'y'), 0...  5.14 us
    ppermute x1, starting transfers between devices, route(): other = lax.ppermute(send, 'c', [(0, 1), (1, 0)])  3.8 us
    pallas_call x1, Pallas kernels, route(): pl.pallas_call(functools.partial(sort_kernel, block), out_shape=(share, s...  3.15 us
    ppermute x3, starting transfers between devices, route(): lax.ppermute(partial[s], 'y', [(i, (i + s) % 4) for i in range(4)])  2.77 us
    pallas_call x1, Pallas kernels, route(): pl.pallas_call(unit_send_kernel, out_shape=(half, shape((ROWS, LANES), f3...  1.98 us
  transfers between devices with their start and end apart: 8, of which 6 were waited for; matrix products, arithmetic and copies ran while one was open for 1% of the time, Pallas kernels for 7%

profile of v1, /device:TPU:1, one launch (start us, length us, event | category | flops | bytes accessed | tf_op | source)
XLA Modules:
  0.0 81.0 jit_solution(9029426446107707529)
XLA Ops:
  0.0 0.0 copy-start.1
  0.0 0.0 copy-start
  0.0 2.0 %unit_send.3 = (bf16[144,2048]{1,0:T(8,128)(2,1)S(1)}, f32[128,128]{1,0:T(8,128)S(1)}) custom-call(f32[128,4096]{1,0:T(8,128)} %x_ref.3, s32[1,128]{1,0:T(1,128)} %bitcast.35), custom_call_target="tpu_custom_call" | custom-call | tf_op jit(solution)/shard_map/unit_send/pallas_call | solution.py:468
  2.0 1.5 %collective-permute-start.7 = (bf16[144,2048]{1,0:T(8,128)(2,1)S(1)}, bf16[144,2048]{1,0:T(8,128)(2,1)S(1)}, u32[]{:S(2)}, u32[]{:S(2)}) collective-permute-start(bf16[144,2048]{1,0:T(8,128)(2,1)S(1)} %get-tuple-element.154), channel_id=1, source_target_pairs={{0,1},{1,0},{2,3},{3,2},{4,5},{5,4},{6,7},{7,6},{8,9},{9,8},{10,11... | collective-permute-start | bytes 1769480 | tf_op jit(solution)/shard_map/ppermute | solution.py:472
  3.5 0.0 copy-done.1
  3.5 0.0 copy-done
  3.5 0.2 unit_keep.3.keep_ref
  3.7 1.4 %collective-permute-done.7.got_ref = bf16[144,2048]{1,0:T(8,128)(2,1)S(1)} collective-permute-done((bf16[144,2048]{1,0:T(8,128)(2,1)S(1)}, bf16[144,2048]{1,0:T(8,128)(2,1)S(1)}, u32[]{:S(2)}, u32[]{:S(2)}) %collective-permute-start.7) | collective-permute-done | bytes 589856 | tf_op jit(solution)/shard_map/ppermute | solution.py:472
  5.1 0.8 %pack.3 = (bf16[64,24,512]{2,1,0:T(8,128)(2,1)S(1)}, s32[8,128]{1,0:T(8,128)S(1)}) custom-call(bf16[144,2048]{1,0:T(8,128)(2,1)S(1)} %unit_keep.3.keep_ref, bf16[144,2048]{1,0:T(8,128)(2,1)S(1)} %collective-permute-done.7.got_ref), custom_call_target="tpu_custom_call" | custom-call | tf_op jit(solution)/shard_map/pack/pallas_call | solution.py:479
  6.0 33.4 %all_to_all.61.x_ref = bf16[64,24,512]{2,1,0:T(8,128)(2,1)S(1)} all-to-all(bf16[64,24,512]{2,1,0:T(8,128)(2,1)S(1)} %get-tuple-element.155), channel_id=1, replica_groups=mesh['x'=4,'z'=4,'y'=4,'c'=2] {'x','z','y'}, dimensions={0} | all-to-all | bytes 3145728 | tf_op jit(solution)/shard_map/all_to_all | solution.py:484
  39.4 1.5 %names.3 = (bf16[64,512]{1,0:T(8,128)(2,1)S(1)}, s32[8,1536]{1,0:T(8,128)S(1)}, s32[64,128]{1,0:T(8,128)S(1)}, s32[64,128]{1,0:T(8,128)S(1)}, s32[8,128]{1,0:T(8,128)S(1)}) custom-call(bf16[64,24,512]{2,1,0:T(8,128)(2,1)S(1)} %all_to_all.61.x_ref), custom_call_target="tpu_custom_call" | custom-call | tf_op jit(solution)/shard_map/names/pallas_call | solution.py:486
  40.9 0.1 collective-permute-start.8
  41.0 3.1 %sort.3 = (bf16[1216,512]{1,0:T(8,128)(2,1)S(1)}, bf16[1216,512]{1,0:T(8,128)(2,1)S(1)}) custom-call(bf16[64,24,512]{2,1,0:T(8,128)(2,1)S(1)} %all_to_all.61.x_ref, s32[8,1536]{1,0:T(8,128)S(1)} %get-tuple-element.158.line_ref), custom_call_target="tpu_custom_call" | custom-call | tf_op jit(solution)/shard_map/sort/pallas_call | solution.py:493
  44.1 0.0 collective-permute-done.8.guest_ref
  44.2 3.8 %collective-permute-start.9 = (bf16[1216,512]{1,0:T(8,128)(2,1)S(1)}, bf16[1216,512]{1,0:T(8,128)(2,1)S(1)}, u32[]{:S(2)}, u32[]{:S(2)}) collective-permute-start(bf16[1216,512]{1,0:T(8,128)(2,1)S(1)} %get-tuple-element.161), channel_id=1, source_target_pairs={{0,1},{1,0},{2,3},{3,2},{4,5},{5,4},{6,7},{7,6},{8,9},{9,8},{10,11... | collective-permute-start | bytes 3735560 | tf_op jit(solution)/shard_map/ppermute | solution.py:498
  48.0 0.0 collective-permute-start.10
  48.0 1.6 %own.3 = (f32[2496,128]{1,0:T(8,128)S(1)}, s32[8,64]{1,0:T(8,128)S(1)}) custom-call(bf16[1216,512]{1,0:T(8,128)(2,1)S(1)} %get-tuple-element.163.x_ref, bf16[64,512]{1,0:T(8,128)(2,1)S(1)} %collective-permute-done.8.guest_ref, s32[64,128]{1,0:T(8,128)S(1)} %get-tuple-element.164.key_ref, s32[64,128]{1,0:T(8,128)S(1)} %get-tuple-element.165.pos_ref), custom_call_target="tpu_custom_call" | custom-call | flops 327155712 | bytes 4194304 | tf_op jit(solution)/shard_map/own/pallas_call | solution.py:500
  49.5 1.1 %collective-permute-done.10.guest_ref = bf16[64,512]{1,0:T(8,128)(2,1)S(1)} collective-permute-done((bf16[64,512]{1,0:T(8,128)(2,1)S(1)}, bf16[64,512]{1,0:T(8,128)(2,1)S(1)}, u32[]{:S(2)}, u32[]{:S(2)}) %collective-permute-start.10) | collective-permute-done | bytes 65568 | tf_op jit(solution)/shard_map/ppermute | solution.py:499
  50.6 0.0 collective-permute-done.9.x_ref
  50.6 1.6 %gram.3 = (f32[352,128]{1,0:T(8,128)S(1)}, f32[352,128]{1,0:T(8,128)S(1)}, f32[352,128]{1,0:T(8,128)S(1)}, f32[352,128]{1,0:T(8,128)S(1)}) custom-call(s32[8,128]{1,0:T(8,128)S(1)} %get-tuple-element.156.meta_ref, bf16[1216,512]{1,0:T(8,128)(2,1)S(1)} %collective-permute-done.9.x_ref, bf16[64,512]{1,0:T(8,128)(2,1)S(1)} %collective-permute-done.10.guest_ref, ...), custom_call_target="tpu_custom_call" | custom-call | tf_op jit(solution)/shard_map/gram/pallas_call | solution.py:507
  52.3 1.2 %collective-permute-start.11 = (f32[352,128]{1,0:T(8,128)S(1)}, f32[352,128]{1,0:T(8,128)S(1)}, u32[]{:S(2)}, u32[]{:S(2)}) collective-permute-start(f32[352,128]{1,0:T(8,128)S(1)} %get-tuple-element.169), channel_id=1, source_target_pairs={{0,4},{2,6},{4,0},{6,2},{1,5},{3,7},{5,1},{7,3},{8,12},{10,14},{12... | collective-permute-start | bytes 540680 | tf_op jit(solution)/shard_map/ppermute | solution.py:515
  53.4 1.6 %collective-permute-start.12 = (f32[352,128]{1,0:T(8,128)S(1)}, f32[352,128]{1,0:T(8,128)S(1)}, u32[]{:S(2)}, u32[]{:S(2)}) collective-permute-start(f32[352,128]{1,0:T(8,128)S(1)} %get-tuple-element.170), channel_id=1, source_target_pairs={{0,6},{2,0},{4,2},{6,4},{1,7},{3,1},{5,3},{7,5},{8,14},{10,8},{12,... | collective-permute-start | bytes 540680 | tf_op jit(solution)/shard_map/ppermute | solution.py:515
  55.0 0.0 collective-permute-start.13
  55.0 0.6 fit.3
  55.6 0.5 slice.6
  56.8 3.1 %collective-permute-done.11.p1 = f32[352,128]{1,0:T(8,128)S(1)} collective-permute-done((f32[352,128]{1,0:T(8,128)S(1)}, f32[352,128]{1,0:T(8,128)S(1)}, u32[]{:S(2)}, u32[]{:S(2)}) %collective-permute-start.11) | collective-permute-done | bytes 180256 | tf_op jit(solution)/shard_map/ppermute | solution.py:515
  59.8 2.2 %collective-permute-done.12.p2 = f32[352,128]{1,0:T(8,128)S(1)} collective-permute-done((f32[352,128]{1,0:T(8,128)S(1)}, f32[352,128]{1,0:T(8,128)S(1)}, u32[]{:S(2)}, u32[]{:S(2)}) %collective-permute-start.12) | collective-permute-done | bytes 180256 | tf_op jit(solution)/shard_map/ppermute | solution.py:515
  62.1 2.1 %collective-permute-done.13.p3 = f32[352,128]{1,0:T(8,128)S(1)} collective-permute-done((f32[352,128]{1,0:T(8,128)S(1)}, f32[352,128]{1,0:T(8,128)S(1)}, u32[]{:S(2)}, u32[]{:S(2)}) %collective-permute-start.13) | collective-permute-done | bytes 180256 | tf_op jit(solution)/shard_map/ppermute | solution.py:515
  64.1 1.5 %maxima.3 = f32[128,128]{1,0:T(8,128)} custom-call(s32[44,128]{1,0:T(8,128)S(1)} %get-tuple-element.174.table_ref, f32[352,128]{1,0:T(8,128)S(1)} %get-tuple-element.175.p0, f32[352,128]{1,0:T(8,128)S(1)} %collective-permute-done.11.p1, f32[352,128]{1,0:T(8,128)S(1)} %collective-permute-done.12.p2, f32[352,128]{1,0:T(8,128)S(1)} %collective-permute-done.13.p3, ...), custom_call_target="tpu_custom_call" | custom-call | tf_op jit(solution)/shard_map/maxima/pallas_call | solution.py:523
  65.6 5.1 %all-to-all-start.8 = ((f32[128,1,128]{2,1,0:T(1,128)}), f32[128,1,128]{2,1,0:T(1,128)S(1)}, u32[]{:S(2)}, u32[]{:S(2)}) async-start(f32[128,1,128]{2,1,0:T(1,128)} %bitcast.17), calls=%async_computation.8 | async-start | bytes 131072 | tf_op jit(solution)/shard_map/all_to_all | solution.py:528
  70.8 9.5 %all-to-all-done.8 = f32[128,1,128]{2,1,0:T(1,128)S(1)} async-done(((f32[128,1,128]{2,1,0:T(1,128)}), f32[128,1,128]{2,1,0:T(1,128)S(1)}, u32[]{:S(2)}, u32[]{:S(2)}) %all-to-all-start.8) | async-done | bytes 65568 | tf_op jit(solution)/shard_map/all_to_all | solution.py:528
  80.2 0.8 pick.3
  (1 shorter events, 0.0 us)
Async XLA Ops:
  0.0 3.5 %copy-start.1 = (f32[128,4096]{1,0:T(8,128)S(1)}, f32[128,4096]{1,0:T(8,128)}, u32[]{:S(2)}) copy-start(f32[128,4096]{1,0:T(8,128)} %x_ref.3) | copy-start | bytes 6291460
  0.0 3.5 %copy-start = (s32[128]{0:T(128)S(1)}, s32[128]{0:T(128)}, u32[]{:S(2)}) copy-start(s32[128]{0:T(128)} %param.9) | copy-start | bytes 1540
  2.0 3.1 %collective-permute-start.7 = (bf16[144,2048]{1,0:T(8,128)(2,1)S(1)}, bf16[144,2048]{1,0:T(8,128)(2,1)S(1)}, u32[]{:S(2)}, u32[]{:S(2)}) collective-permute-start(bf16[144,2048]{1,0:T(8,128)(2,1)S(1)} %get-tuple-element.154), channel_id=1, source_target_pairs={{0,1},{1,0},{2,3},{3,2},{4,5},{5,4},{6,7},{7,6},{8,9},{9,8},{10,11... | collective-permute-start | bytes 1769480 | tf_op jit(solution)/shard_map/ppermute | solution.py:472
  40.9 3.2 %collective-permute-start.8 = (bf16[64,512]{1,0:T(8,128)(2,1)S(1)}, bf16[64,512]{1,0:T(8,128)(2,1)S(1)}, u32[]{:S(2)}, u32[]{:S(2)}) collective-permute-start(bf16[64,512]{1,0:T(8,128)(2,1)S(1)} %get-tuple-element.157), channel_id=1, source_target_pairs={{0,24},{8,0},{16,8},{24,16},{1,25},{9,1},{17,9},{25,17},{2,26},{10... | collective-permute-start | bytes 196616 | tf_op jit(solution)/shard_map/ppermute | solution.py:491
  44.2 6.5 %collective-permute-start.9 = (bf16[1216,512]{1,0:T(8,128)(2,1)S(1)}, bf16[1216,512]{1,0:T(8,128)(2,1)S(1)}, u32[]{:S(2)}, u32[]{:S(2)}) collective-permute-start(bf16[1216,512]{1,0:T(8,128)(2,1)S(1)} %get-tuple-element.161), channel_id=1, source_target_pairs={{0,1},{1,0},{2,3},{3,2},{4,5},{5,4},{6,7},{7,6},{8,9},{9,8},{10,11... | collective-permute-start | bytes 3735560 | tf_op jit(solution)/shard_map/ppermute | solution.py:498
  48.0 2.7 %collective-permute-start.10 = (bf16[64,512]{1,0:T(8,128)(2,1)S(1)}, bf16[64,512]{1,0:T(8,128)(2,1)S(1)}, u32[]{:S(2)}, u32[]{:S(2)}) collective-permute-start(bf16[64,512]{1,0:T(8,128)(2,1)S(1)} %collective-permute-done.8.guest_ref), channel_id=1, source_target_pairs={{0,1},{1,0},{2,3},{3,2},{4,5},{5,4},{6,7},{7,6},{8,9},{9,8},{10,11... | collective-permute-start | bytes 196616 | tf_op jit(solution)/shard_map/ppermute | solution.py:499
  52.3 7.6 %collective-permute-start.11 = (f32[352,128]{1,0:T(8,128)S(1)}, f32[352,128]{1,0:T(8,128)S(1)}, u32[]{:S(2)}, u32[]{:S(2)}) collective-permute-start(f32[352,128]{1,0:T(8,128)S(1)} %get-tuple-element.169), channel_id=1, source_target_pairs={{0,4},{2,6},{4,0},{6,2},{1,5},{3,7},{5,1},{7,3},{8,12},{10,14},{12... | collective-permute-start | bytes 540680 | tf_op jit(solution)/shard_map/ppermute | solution.py:515
  53.4 8.6 %collective-permute-start.12 = (f32[352,128]{1,0:T(8,128)S(1)}, f32[352,128]{1,0:T(8,128)S(1)}, u32[]{:S(2)}, u32[]{:S(2)}) collective-permute-start(f32[352,128]{1,0:T(8,128)S(1)} %get-tuple-element.170), channel_id=1, source_target_pairs={{0,6},{2,0},{4,2},{6,4},{1,7},{3,1},{5,3},{7,5},{8,14},{10,8},{12,... | collective-permute-start | bytes 540680 | tf_op jit(solution)/shard_map/ppermute | solution.py:515
  55.0 9.1 %collective-permute-start.13 = (f32[352,128]{1,0:T(8,128)S(1)}, f32[352,128]{1,0:T(8,128)S(1)}, u32[]{:S(2)}, u32[]{:S(2)}) collective-permute-start(f32[352,128]{1,0:T(8,128)S(1)} %get-tuple-element.171), channel_id=1, source_target_pairs={{0,2},{2,4},{4,6},{6,0},{1,3},{3,5},{5,7},{7,1},{8,10},{10,12},{12... | collective-permute-start | bytes 540680 | tf_op jit(solution)/shard_map/ppermute | solution.py:515
  65.6 14.6 %all-to-all-start.8 = ((f32[128,1,128]{2,1,0:T(1,128)}), f32[128,1,128]{2,1,0:T(1,128)S(1)}, u32[]{:S(2)}, u32[]{:S(2)}) async-start(f32[128,1,128]{2,1,0:T(1,128)} %bitcast.17), calls=%async_computation.8 | async-start | bytes 131072 | tf_op jit(solution)/shard_map/all_to_all | solution.py:528

commit v2 on v1

--- a/solution.py
+++ b/solution.py
@@ -403,18 +403,16 @@
 
 
 def pick_kernel(v_ref, code_ref, out_ref):
-    c = index_on("c")
     values = jnp.maximum(v_ref[:CHIPS, :], v_ref[CHIPS:, :])
     values = jnp.max(values.reshape(BINS, 4, LANES), axis=1)
-    eye = iota((LANES, LANES), 0) == iota((LANES, LANES), 1)
-    code = jnp.max(jnp.where(iota((8, ROWS), 0) == c, code_ref[...], -1), axis=0, keepdims=True)
-    code = jnp.max(jnp.where(eye, code.astype(f32), -1.0), axis=1, keepdims=True).astype(i32)
-    slot = iota((ROWS, LANES), 1)
-    best = jnp.full((ROWS, LANES), -1.0, f32)
+    code = jnp.max(jnp.where(iota((8, ROWS), 0) == index_on("c"), code_ref[...], -1), axis=0, keepdims=True)
+    code = jnp.broadcast_to(code, (8, ROWS))
+    row, lane = code >> 7, code & (LANES - 1)
+    best = jnp.full((8, ROWS), -1.0, f32)
     for b in range(BINS):
-        best = jnp.where(slot + b * LANES == code, values[b:b + 1], best)
-    best = jnp.max(best, axis=1, keepdims=True)
-    out_ref[...] = jnp.max(jnp.where(eye, best, -1.0), axis=0, keepdims=True)
+        value = jnp.broadcast_to(values[b:b + 1], (8, ROWS))
+        best = jnp.where(row == b, jnp.take_along_axis(value, lane, axis=1, mode="promise_in_bounds"), best)
+    out_ref[...] = best[:1]
 
 
 def gather_groups(embeddings, cluster_ids):

time: 81.2 us -> 81 us (level)
  no operation moved by 1% of the time
where the time goes in v2:
time: 81 us; the launch traced here: 80.9 us
  blocking collectives  33.4 us (41%)
  waiting for transfers between devices  19.3 us (24%)
  Pallas kernels  13.6 us (17%)
  starting transfers between devices  13.3 us (16%)
    all_to_all x1, blocking collectives, route(): packed = lax.all_to_all(packed, ('x', 'z', 'y'), 0, 0, tiled=True)  33.4 us
    all_to_all x1, waiting for transfers between devices, route(): lax.all_to_all(best.reshape(2 * CHIPS, 1, LANES), ('c', 'x', 'z', 'y'), 0...  9.47 us
    ppermute x3, waiting for transfers between devices, route(): lax.ppermute(partial[s], 'y', [(i, (i + s) % 4) for i in range(4)])  7.35 us
    all_to_all x1, starting transfers between devices, route(): lax.all_to_all(best.reshape(2 * CHIPS, 1, LANES), ('c', 'x', 'z', 'y'), 0...  5.14 us
    ppermute x1, starting transfers between devices, route(): other = lax.ppermute(send, 'c', [(0, 1), (1, 0)])  3.8 us
    pallas_call x1, Pallas kernels, route(): pl.pallas_call(functools.partial(sort_kernel, block), out_shape=(share, s...  3.15 us
    ppermute x3, starting transfers between devices, route(): lax.ppermute(partial[s], 'y', [(i, (i + s) % 4) for i in range(4)])  2.77 us
    pallas_call x1, Pallas kernels, route(): pl.pallas_call(unit_send_kernel, out_shape=(half, shape((ROWS, LANES), f3...  1.98 us
  transfers between devices with their start and end apart: 8, of which 6 were waited for; matrix products, arithmetic and copies ran while one was open for 1% of the time, Pallas kernels for 7%

profile of v2, /device:TPU:1, one launch (start us, length us, event | category | flops | bytes accessed | tf_op | source)
XLA Modules:
  0.0 80.9 jit_solution(16062213655532964218)
XLA Ops:
  0.0 0.0 copy-start.1
  0.0 0.0 copy-start
  0.0 2.0 %unit_send.3 = (bf16[144,2048]{1,0:T(8,128)(2,1)S(1)}, f32[128,128]{1,0:T(8,128)S(1)}) custom-call(f32[128,4096]{1,0:T(8,128)} %x_ref.3, s32[1,128]{1,0:T(1,128)} %bitcast.35), custom_call_target="tpu_custom_call" | custom-call | tf_op jit(solution)/shard_map/unit_send/pallas_call | solution.py:466
  2.0 1.5 %collective-permute-start.7 = (bf16[144,2048]{1,0:T(8,128)(2,1)S(1)}, bf16[144,2048]{1,0:T(8,128)(2,1)S(1)}, u32[]{:S(2)}, u32[]{:S(2)}) collective-permute-start(bf16[144,2048]{1,0:T(8,128)(2,1)S(1)} %get-tuple-element.154), channel_id=1, source_target_pairs={{0,1},{1,0},{2,3},{3,2},{4,5},{5,4},{6,7},{7,6},{8,9},{9,8},{10,11... | collective-permute-start | bytes 1769480 | tf_op jit(solution)/shard_map/ppermute | solution.py:470
  3.5 0.0 copy-done.1
  3.5 0.0 copy-done
  3.5 0.2 unit_keep.3.keep_ref
  3.7 1.4 %collective-permute-done.7.got_ref = bf16[144,2048]{1,0:T(8,128)(2,1)S(1)} collective-permute-done((bf16[144,2048]{1,0:T(8,128)(2,1)S(1)}, bf16[144,2048]{1,0:T(8,128)(2,1)S(1)}, u32[]{:S(2)}, u32[]{:S(2)}) %collective-permute-start.7) | collective-permute-done | bytes 589856 | tf_op jit(solution)/shard_map/ppermute | solution.py:470
  5.1 0.8 %pack.3 = (bf16[64,24,512]{2,1,0:T(8,128)(2,1)S(1)}, s32[8,128]{1,0:T(8,128)S(1)}) custom-call(bf16[144,2048]{1,0:T(8,128)(2,1)S(1)} %unit_keep.3.keep_ref, bf16[144,2048]{1,0:T(8,128)(2,1)S(1)} %collective-permute-done.7.got_ref), custom_call_target="tpu_custom_call" | custom-call | tf_op jit(solution)/shard_map/pack/pallas_call | solution.py:477
  6.0 33.4 %all_to_all.61.x_ref = bf16[64,24,512]{2,1,0:T(8,128)(2,1)S(1)} all-to-all(bf16[64,24,512]{2,1,0:T(8,128)(2,1)S(1)} %get-tuple-element.155), channel_id=1, replica_groups=mesh['x'=4,'z'=4,'y'=4,'c'=2] {'x','z','y'}, dimensions={0} | all-to-all | bytes 3145728 | tf_op jit(solution)/shard_map/all_to_all | solution.py:482
  39.4 1.5 %names.3 = (bf16[64,512]{1,0:T(8,128)(2,1)S(1)}, s32[8,1536]{1,0:T(8,128)S(1)}, s32[64,128]{1,0:T(8,128)S(1)}, s32[64,128]{1,0:T(8,128)S(1)}, s32[8,128]{1,0:T(8,128)S(1)}) custom-call(bf16[64,24,512]{2,1,0:T(8,128)(2,1)S(1)} %all_to_all.61.x_ref), custom_call_target="tpu_custom_call" | custom-call | tf_op jit(solution)/shard_map/names/pallas_call | solution.py:484
  40.9 0.1 collective-permute-start.8
  41.0 3.1 %sort.3 = (bf16[1216,512]{1,0:T(8,128)(2,1)S(1)}, bf16[1216,512]{1,0:T(8,128)(2,1)S(1)}) custom-call(bf16[64,24,512]{2,1,0:T(8,128)(2,1)S(1)} %all_to_all.61.x_ref, s32[8,1536]{1,0:T(8,128)S(1)} %get-tuple-element.158.line_ref), custom_call_target="tpu_custom_call" | custom-call | tf_op jit(solution)/shard_map/sort/pallas_call | solution.py:491
  44.1 0.0 collective-permute-done.8.guest_ref
  44.2 3.8 %collective-permute-start.9 = (bf16[1216,512]{1,0:T(8,128)(2,1)S(1)}, bf16[1216,512]{1,0:T(8,128)(2,1)S(1)}, u32[]{:S(2)}, u32[]{:S(2)}) collective-permute-start(bf16[1216,512]{1,0:T(8,128)(2,1)S(1)} %get-tuple-element.161), channel_id=1, source_target_pairs={{0,1},{1,0},{2,3},{3,2},{4,5},{5,4},{6,7},{7,6},{8,9},{9,8},{10,11... | collective-permute-start | bytes 3735560 | tf_op jit(solution)/shard_map/ppermute | solution.py:496
  48.0 0.0 collective-permute-start.10
  48.0 1.6 %own.3 = (f32[2496,128]{1,0:T(8,128)S(1)}, s32[8,64]{1,0:T(8,128)S(1)}) custom-call(bf16[1216,512]{1,0:T(8,128)(2,1)S(1)} %get-tuple-element.163.x_ref, bf16[64,512]{1,0:T(8,128)(2,1)S(1)} %collective-permute-done.8.guest_ref, s32[64,128]{1,0:T(8,128)S(1)} %get-tuple-element.164.key_ref, s32[64,128]{1,0:T(8,128)S(1)} %get-tuple-element.165.pos_ref), custom_call_target="tpu_custom_call" | custom-call | flops 327155712 | bytes 4194304 | tf_op jit(solution)/shard_map/own/pallas_call | solution.py:498
  49.5 1.1 %collective-permute-done.10.guest_ref = bf16[64,512]{1,0:T(8,128)(2,1)S(1)} collective-permute-done((bf16[64,512]{1,0:T(8,128)(2,1)S(1)}, bf16[64,512]{1,0:T(8,128)(2,1)S(1)}, u32[]{:S(2)}, u32[]{:S(2)}) %collective-permute-start.10) | collective-permute-done | bytes 65568 | tf_op jit(solution)/shard_map/ppermute | solution.py:497
  50.6 0.0 collective-permute-done.9.x_ref
  50.6 1.6 %gram.3 = (f32[352,128]{1,0:T(8,128)S(1)}, f32[352,128]{1,0:T(8,128)S(1)}, f32[352,128]{1,0:T(8,128)S(1)}, f32[352,128]{1,0:T(8,128)S(1)}) custom-call(s32[8,128]{1,0:T(8,128)S(1)} %get-tuple-element.156.meta_ref, bf16[1216,512]{1,0:T(8,128)(2,1)S(1)} %collective-permute-done.9.x_ref, bf16[64,512]{1,0:T(8,128)(2,1)S(1)} %collective-permute-done.10.guest_ref, ...), custom_call_target="tpu_custom_call" | custom-call | tf_op jit(solution)/shard_map/gram/pallas_call | solution.py:505
  52.3 1.2 %collective-permute-start.11 = (f32[352,128]{1,0:T(8,128)S(1)}, f32[352,128]{1,0:T(8,128)S(1)}, u32[]{:S(2)}, u32[]{:S(2)}) collective-permute-start(f32[352,128]{1,0:T(8,128)S(1)} %get-tuple-element.169), channel_id=1, source_target_pairs={{0,4},{2,6},{4,0},{6,2},{1,5},{3,7},{5,1},{7,3},{8,12},{10,14},{12... | collective-permute-start | bytes 540680 | tf_op jit(solution)/shard_map/ppermute | solution.py:513
  53.4 1.6 %collective-permute-start.12 = (f32[352,128]{1,0:T(8,128)S(1)}, f32[352,128]{1,0:T(8,128)S(1)}, u32[]{:S(2)}, u32[]{:S(2)}) collective-permute-start(f32[352,128]{1,0:T(8,128)S(1)} %get-tuple-element.170), channel_id=1, source_target_pairs={{0,6},{2,0},{4,2},{6,4},{1,7},{3,1},{5,3},{7,5},{8,14},{10,8},{12,... | collective-permute-start | bytes 540680 | tf_op jit(solution)/shard_map/ppermute | solution.py:513
  55.0 0.0 collective-permute-start.13
  55.0 0.6 fit.3
  55.6 0.5 slice.6
  56.8 3.1 %collective-permute-done.11.p1 = f32[352,128]{1,0:T(8,128)S(1)} collective-permute-done((f32[352,128]{1,0:T(8,128)S(1)}, f32[352,128]{1,0:T(8,128)S(1)}, u32[]{:S(2)}, u32[]{:S(2)}) %collective-permute-start.11) | collective-permute-done | bytes 180256 | tf_op jit(solution)/shard_map/ppermute | solution.py:513
  59.8 2.2 %collective-permute-done.12.p2 = f32[352,128]{1,0:T(8,128)S(1)} collective-permute-done((f32[352,128]{1,0:T(8,128)S(1)}, f32[352,128]{1,0:T(8,128)S(1)}, u32[]{:S(2)}, u32[]{:S(2)}) %collective-permute-start.12) | collective-permute-done | bytes 180256 | tf_op jit(solution)/shard_map/ppermute | solution.py:513
  62.1 2.1 %collective-permute-done.13.p3 = f32[352,128]{1,0:T(8,128)S(1)} collective-permute-done((f32[352,128]{1,0:T(8,128)S(1)}, f32[352,128]{1,0:T(8,128)S(1)}, u32[]{:S(2)}, u32[]{:S(2)}) %collective-permute-start.13) | collective-permute-done | bytes 180256 | tf_op jit(solution)/shard_map/ppermute | solution.py:513
  64.1 1.5 %maxima.3 = f32[128,128]{1,0:T(8,128)} custom-call(s32[44,128]{1,0:T(8,128)S(1)} %get-tuple-element.174.table_ref, f32[352,128]{1,0:T(8,128)S(1)} %get-tuple-element.175.p0, f32[352,128]{1,0:T(8,128)S(1)} %collective-permute-done.11.p1, f32[352,128]{1,0:T(8,128)S(1)} %collective-permute-done.12.p2, f32[352,128]{1,0:T(8,128)S(1)} %collective-permute-done.13.p3, ...), custom_call_target="tpu_custom_call" | custom-call | tf_op jit(solution)/shard_map/maxima/pallas_call | solution.py:521
  65.6 5.1 %all-to-all-start.8 = ((f32[128,1,128]{2,1,0:T(1,128)}), f32[128,1,128]{2,1,0:T(1,128)S(1)}, u32[]{:S(2)}, u32[]{:S(2)}) async-start(f32[128,1,128]{2,1,0:T(1,128)} %bitcast.17), calls=%async_computation.8 | async-start | bytes 131072 | tf_op jit(solution)/shard_map/all_to_all | solution.py:526
  70.8 9.5 %all-to-all-done.8 = f32[128,1,128]{2,1,0:T(1,128)S(1)} async-done(((f32[128,1,128]{2,1,0:T(1,128)}), f32[128,1,128]{2,1,0:T(1,128)S(1)}, u32[]{:S(2)}, u32[]{:S(2)}) %all-to-all-start.8) | async-done | bytes 65568 | tf_op jit(solution)/shard_map/all_to_all | solution.py:526
  80.2 0.6 pick.3
  (1 shorter events, 0.0 us)
Async XLA Ops:
  0.0 3.5 %copy-start.1 = (f32[128,4096]{1,0:T(8,128)S(1)}, f32[128,4096]{1,0:T(8,128)}, u32[]{:S(2)}) copy-start(f32[128,4096]{1,0:T(8,128)} %x_ref.3) | copy-start | bytes 6291460
  0.0 3.5 %copy-start = (s32[128]{0:T(128)S(1)}, s32[128]{0:T(128)}, u32[]{:S(2)}) copy-start(s32[128]{0:T(128)} %param.9) | copy-start | bytes 1540
  2.0 3.1 %collective-permute-start.7 = (bf16[144,2048]{1,0:T(8,128)(2,1)S(1)}, bf16[144,2048]{1,0:T(8,128)(2,1)S(1)}, u32[]{:S(2)}, u32[]{:S(2)}) collective-permute-start(bf16[144,2048]{1,0:T(8,128)(2,1)S(1)} %get-tuple-element.154), channel_id=1, source_target_pairs={{0,1},{1,0},{2,3},{3,2},{4,5},{5,4},{6,7},{7,6},{8,9},{9,8},{10,11... | collective-permute-start | bytes 1769480 | tf_op jit(solution)/shard_map/ppermute | solution.py:470
  40.9 3.2 %collective-permute-start.8 = (bf16[64,512]{1,0:T(8,128)(2,1)S(1)}, bf16[64,512]{1,0:T(8,128)(2,1)S(1)}, u32[]{:S(2)}, u32[]{:S(2)}) collective-permute-start(bf16[64,512]{1,0:T(8,128)(2,1)S(1)} %get-tuple-element.157), channel_id=1, source_target_pairs={{0,24},{8,0},{16,8},{24,16},{1,25},{9,1},{17,9},{25,17},{2,26},{10... | collective-permute-start | bytes 196616 | tf_op jit(solution)/shard_map/ppermute | solution.py:489
  44.2 6.5 %collective-permute-start.9 = (bf16[1216,512]{1,0:T(8,128)(2,1)S(1)}, bf16[1216,512]{1,0:T(8,128)(2,1)S(1)}, u32[]{:S(2)}, u32[]{:S(2)}) collective-permute-start(bf16[1216,512]{1,0:T(8,128)(2,1)S(1)} %get-tuple-element.161), channel_id=1, source_target_pairs={{0,1},{1,0},{2,3},{3,2},{4,5},{5,4},{6,7},{7,6},{8,9},{9,8},{10,11... | collective-permute-start | bytes 3735560 | tf_op jit(solution)/shard_map/ppermute | solution.py:496
  48.0 2.7 %collective-permute-start.10 = (bf16[64,512]{1,0:T(8,128)(2,1)S(1)}, bf16[64,512]{1,0:T(8,128)(2,1)S(1)}, u32[]{:S(2)}, u32[]{:S(2)}) collective-permute-start(bf16[64,512]{1,0:T(8,128)(2,1)S(1)} %collective-permute-done.8.guest_ref), channel_id=1, source_target_pairs={{0,1},{1,0},{2,3},{3,2},{4,5},{5,4},{6,7},{7,6},{8,9},{9,8},{10,11... | collective-permute-start | bytes 196616 | tf_op jit(solution)/shard_map/ppermute | solution.py:497
  52.3 7.6 %collective-permute-start.11 = (f32[352,128]{1,0:T(8,128)S(1)}, f32[352,128]{1,0:T(8,128)S(1)}, u32[]{:S(2)}, u32[]{:S(2)}) collective-permute-start(f32[352,128]{1,0:T(8,128)S(1)} %get-tuple-element.169), channel_id=1, source_target_pairs={{0,4},{2,6},{4,0},{6,2},{1,5},{3,7},{5,1},{7,3},{8,12},{10,14},{12... | collective-permute-start | bytes 540680 | tf_op jit(solution)/shard_map/ppermute | solution.py:513
  53.4 8.7 %collective-permute-start.12 = (f32[352,128]{1,0:T(8,128)S(1)}, f32[352,128]{1,0:T(8,128)S(1)}, u32[]{:S(2)}, u32[]{:S(2)}) collective-permute-start(f32[352,128]{1,0:T(8,128)S(1)} %get-tuple-element.170), channel_id=1, source_target_pairs={{0,6},{2,0},{4,2},{6,4},{1,7},{3,1},{5,3},{7,5},{8,14},{10,8},{12,... | collective-permute-start | bytes 540680 | tf_op jit(solution)/shard_map/ppermute | solution.py:513
  55.0 9.1 %collective-permute-start.13 = (f32[352,128]{1,0:T(8,128)S(1)}, f32[352,128]{1,0:T(8,128)S(1)}, u32[]{:S(2)}, u32[]{:S(2)}) collective-permute-start(f32[352,128]{1,0:T(8,128)S(1)} %get-tuple-element.171), channel_id=1, source_target_pairs={{0,2},{2,4},{4,6},{6,0},{1,3},{3,5},{5,7},{7,1},{8,10},{10,12},{12... | collective-permute-start | bytes 540680 | tf_op jit(solution)/shard_map/ppermute | solution.py:513
  65.6 14.6 %all-to-all-start.8 = ((f32[128,1,128]{2,1,0:T(1,128)}), f32[128,1,128]{2,1,0:T(1,128)S(1)}, u32[]{:S(2)}, u32[]{:S(2)}) async-start(f32[128,1,128]{2,1,0:T(1,128)} %bitcast.17), calls=%async_computation.8 | async-start | bytes 131072 | tf_op jit(solution)/shard_map/all_to_all | solution.py:526

commit v3 on v2

--- a/solution.py
+++ b/solution.py
@@ -385,9 +385,7 @@
         along = jnp.max(one, axis=1, keepdims=True)
         along = jnp.max(jnp.where(sub + offset == lane, along, -1.0), axis=0, keepdims=True)
         best = jnp.maximum(best, jnp.where(row == unit_row, along, -1.0))
-        along = jnp.max(two, axis=1, keepdims=True)
-        two = jnp.maximum(jnp.where(sub == lane, along, -1.0), pltpu.roll(two, UNIT, 1))
-        down = jnp.max(jnp.maximum(one, two), axis=0, keepdims=True)
+        down = jnp.max(jnp.maximum(one, pltpu.roll(two, UNIT, 1)), axis=0, keepdims=True)
         best = jnp.maximum(best, jnp.where(row == col, down, -1.0))
     pos = pos_ref[...]
     pos = jnp.where(pos >= STARTS[1], pos + 64, pos)
@@ -510,7 +508,7 @@
         compiler_params=params(16), name="gram",
     )(meta, other, swapped, far, raw)
     arrived = [partial[0]] + [
-        lax.ppermute(partial[s], "y", [(i, (i + s) % 4) for i in range(4)]) for s in (2, 3, 1)
+        lax.ppermute(partial[s], "y", [(i, (i + s) % 4) for i in range(4)]) for s in (3, 2, 1)
     ]
     over, table = pl.pallas_call(
         functools.partial(fit_kernel, block, units),

time: 81 us -> 82.1 us (1.014)
  waiting for transfers between devices: 19.3 us -> 20.7 us
    ppermute x3, waiting for transfers between devices: 7.35 us -> 8.74 us  [route(): lax.ppermute(partial[s], 'y', [(i, (i + s) % 4) for i in range(4)])]
where the time goes in v3:
time: 82.1 us; the launch traced here: 81.9 us
  blocking collectives  33.4 us (41%)
  waiting for transfers between devices  20.7 us (25%)
  Pallas kernels  13.5 us (16%)
  starting transfers between devices  13 us (16%)
    all_to_all x1, blocking collectives, route(): packed = lax.all_to_all(packed, ('x', 'z', 'y'), 0, 0, tiled=True)  33.4 us
    all_to_all x1, waiting for transfers between devices, route(): lax.all_to_all(best.reshape(2 * CHIPS, 1, LANES), ('c', 'x', 'z', 'y'), 0...  9.47 us
    ppermute x3, waiting for transfers between devices, route(): lax.ppermute(partial[s], 'y', [(i, (i + s) % 4) for i in range(4)])  8.74 us
    all_to_all x1, starting transfers between devices, route(): lax.all_to_all(best.reshape(2 * CHIPS, 1, LANES), ('c', 'x', 'z', 'y'), 0...  5.46 us
    ppermute x1, starting transfers between devices, route(): other = lax.ppermute(send, 'c', [(0, 1), (1, 0)])  3.8 us
    pallas_call x1, Pallas kernels, route(): pl.pallas_call(functools.partial(sort_kernel, block), out_shape=(share, s...  3.15 us
    ppermute x3, starting transfers between devices, route(): lax.ppermute(partial[s], 'y', [(i, (i + s) % 4) for i in range(4)])  2.15 us
    pallas_call x1, Pallas kernels, route(): pl.pallas_call(unit_send_kernel, out_shape=(half, shape((ROWS, LANES), f3...  1.98 us
  transfers between devices with their start and end apart: 8, of which 6 were waited for; matrix products, arithmetic and copies ran while one was open for 1% of the time, Pallas kernels for 7%

profile of v3, /device:TPU:1, one launch (start us, length us, event | category | flops | bytes accessed | tf_op | source)
XLA Modules:
  0.0 81.9 jit_solution(4477471286816787082)
XLA Ops:
  0.0 0.0 copy-start.1
  0.0 0.0 copy-start
  0.0 2.0 %unit_send.3 = (bf16[144,2048]{1,0:T(8,128)(2,1)S(1)}, f32[128,128]{1,0:T(8,128)S(1)}) custom-call(f32[128,4096]{1,0:T(8,128)} %x_ref.3, s32[1,128]{1,0:T(1,128)} %bitcast.35), custom_call_target="tpu_custom_call" | custom-call | tf_op jit(solution)/shard_map/unit_send/pallas_call | solution.py:464
  2.0 1.5 %collective-permute-start.7 = (bf16[144,2048]{1,0:T(8,128)(2,1)S(1)}, bf16[144,2048]{1,0:T(8,128)(2,1)S(1)}, u32[]{:S(2)}, u32[]{:S(2)}) collective-permute-start(bf16[144,2048]{1,0:T(8,128)(2,1)S(1)} %get-tuple-element.154), channel_id=1, source_target_pairs={{0,1},{1,0},{2,3},{3,2},{4,5},{5,4},{6,7},{7,6},{8,9},{9,8},{10,11... | collective-permute-start | bytes 1769480 | tf_op jit(solution)/shard_map/ppermute | solution.py:468
  3.5 0.0 copy-done.1
  3.5 0.0 copy-done
  3.5 0.2 unit_keep.3.keep_ref
  3.7 1.4 %collective-permute-done.7.got_ref = bf16[144,2048]{1,0:T(8,128)(2,1)S(1)} collective-permute-done((bf16[144,2048]{1,0:T(8,128)(2,1)S(1)}, bf16[144,2048]{1,0:T(8,128)(2,1)S(1)}, u32[]{:S(2)}, u32[]{:S(2)}) %collective-permute-start.7) | collective-permute-done | bytes 589856 | tf_op jit(solution)/shard_map/ppermute | solution.py:468
  5.1 0.8 %pack.3 = (bf16[64,24,512]{2,1,0:T(8,128)(2,1)S(1)}, s32[8,128]{1,0:T(8,128)S(1)}) custom-call(bf16[144,2048]{1,0:T(8,128)(2,1)S(1)} %unit_keep.3.keep_ref, bf16[144,2048]{1,0:T(8,128)(2,1)S(1)} %collective-permute-done.7.got_ref), custom_call_target="tpu_custom_call" | custom-call | tf_op jit(solution)/shard_map/pack/pallas_call | solution.py:475
  6.0 33.4 %all_to_all.61.x_ref = bf16[64,24,512]{2,1,0:T(8,128)(2,1)S(1)} all-to-all(bf16[64,24,512]{2,1,0:T(8,128)(2,1)S(1)} %get-tuple-element.155), channel_id=1, replica_groups=mesh['x'=4,'z'=4,'y'=4,'c'=2] {'x','z','y'}, dimensions={0} | all-to-all | bytes 3145728 | tf_op jit(solution)/shard_map/all_to_all | solution.py:480
  39.4 1.5 %names.3 = (bf16[64,512]{1,0:T(8,128)(2,1)S(1)}, s32[8,1536]{1,0:T(8,128)S(1)}, s32[64,128]{1,0:T(8,128)S(1)}, s32[64,128]{1,0:T(8,128)S(1)}, s32[8,128]{1,0:T(8,128)S(1)}) custom-call(bf16[64,24,512]{2,1,0:T(8,128)(2,1)S(1)} %all_to_all.61.x_ref), custom_call_target="tpu_custom_call" | custom-call | tf_op jit(solution)/shard_map/names/pallas_call | solution.py:482
  40.9 0.1 collective-permute-start.8
  41.0 3.1 %sort.3 = (bf16[1216,512]{1,0:T(8,128)(2,1)S(1)}, bf16[1216,512]{1,0:T(8,128)(2,1)S(1)}) custom-call(bf16[64,24,512]{2,1,0:T(8,128)(2,1)S(1)} %all_to_all.61.x_ref, s32[8,1536]{1,0:T(8,128)S(1)} %get-tuple-element.158.line_ref), custom_call_target="tpu_custom_call" | custom-call | tf_op jit(solution)/shard_map/sort/pallas_call | solution.py:489
  44.1 0.0 collective-permute-done.8.guest_ref
  44.2 3.8 %collective-permute-start.9 = (bf16[1216,512]{1,0:T(8,128)(2,1)S(1)}, bf16[1216,512]{1,0:T(8,128)(2,1)S(1)}, u32[]{:S(2)}, u32[]{:S(2)}) collective-permute-start(bf16[1216,512]{1,0:T(8,128)(2,1)S(1)} %get-tuple-element.161), channel_id=1, source_target_pairs={{0,1},{1,0},{2,3},{3,2},{4,5},{5,4},{6,7},{7,6},{8,9},{9,8},{10,11... | collective-permute-start | bytes 3735560 | tf_op jit(solution)/shard_map/ppermute | solution.py:494
  48.0 0.0 collective-permute-start.10
  48.0 1.6 %own.3 = (f32[2496,128]{1,0:T(8,128)S(1)}, s32[8,64]{1,0:T(8,128)S(1)}) custom-call(bf16[1216,512]{1,0:T(8,128)(2,1)S(1)} %get-tuple-element.163.x_ref, bf16[64,512]{1,0:T(8,128)(2,1)S(1)} %collective-permute-done.8.guest_ref, s32[64,128]{1,0:T(8,128)S(1)} %get-tuple-element.164.key_ref, s32[64,128]{1,0:T(8,128)S(1)} %get-tuple-element.165.pos_ref), custom_call_target="tpu_custom_call" | custom-call | flops 327155712 | bytes 4194304 | tf_op jit(solution)/shard_map/own/pallas_call | solution.py:496
  49.5 1.1 %collective-permute-done.10.guest_ref = bf16[64,512]{1,0:T(8,128)(2,1)S(1)} collective-permute-done((bf16[64,512]{1,0:T(8,128)(2,1)S(1)}, bf16[64,512]{1,0:T(8,128)(2,1)S(1)}, u32[]{:S(2)}, u32[]{:S(2)}) %collective-permute-start.10) | collective-permute-done | bytes 65568 | tf_op jit(solution)/shard_map/ppermute | solution.py:495
  50.6 0.0 collective-permute-done.9.x_ref
  50.6 1.6 %gram.3 = (f32[352,128]{1,0:T(8,128)S(1)}, f32[352,128]{1,0:T(8,128)S(1)}, f32[352,128]{1,0:T(8,128)S(1)}, f32[352,128]{1,0:T(8,128)S(1)}) custom-call(s32[8,128]{1,0:T(8,128)S(1)} %get-tuple-element.156.meta_ref, bf16[1216,512]{1,0:T(8,128)(2,1)S(1)} %collective-permute-done.9.x_ref, bf16[64,512]{1,0:T(8,128)(2,1)S(1)} %collective-permute-done.10.guest_ref, ...), custom_call_target="tpu_custom_call" | custom-call | tf_op jit(solution)/shard_map/gram/pallas_call | solution.py:503
  52.3 0.8 collective-permute-start.11
  53.1 1.3 %collective-permute-start.12 = (f32[352,128]{1,0:T(8,128)S(1)}, f32[352,128]{1,0:T(8,128)S(1)}, u32[]{:S(2)}, u32[]{:S(2)}) collective-permute-start(f32[352,128]{1,0:T(8,128)S(1)} %get-tuple-element.170), channel_id=1, source_target_pairs={{0,4},{2,6},{4,0},{6,2},{1,5},{3,7},{5,1},{7,3},{8,12},{10,14},{12... | collective-permute-start | bytes 540680 | tf_op jit(solution)/shard_map/ppermute | solution.py:511
  54.4 0.0 collective-permute-start.13
  54.4 0.6 fit.3
  55.0 0.5 slice.6
  56.2 2.2 %collective-permute-done.11.p1 = f32[352,128]{1,0:T(8,128)S(1)} collective-permute-done((f32[352,128]{1,0:T(8,128)S(1)}, f32[352,128]{1,0:T(8,128)S(1)}, u32[]{:S(2)}, u32[]{:S(2)}) %collective-permute-start.11) | collective-permute-done | bytes 180256 | tf_op jit(solution)/shard_map/ppermute | solution.py:511
  58.3 2.0 %collective-permute-done.12.p2 = f32[352,128]{1,0:T(8,128)S(1)} collective-permute-done((f32[352,128]{1,0:T(8,128)S(1)}, f32[352,128]{1,0:T(8,128)S(1)}, u32[]{:S(2)}, u32[]{:S(2)}) %collective-permute-start.12) | collective-permute-done | bytes 180256 | tf_op jit(solution)/shard_map/ppermute | solution.py:511
  60.3 4.6 %collective-permute-done.13.p3 = f32[352,128]{1,0:T(8,128)S(1)} collective-permute-done((f32[352,128]{1,0:T(8,128)S(1)}, f32[352,128]{1,0:T(8,128)S(1)}, u32[]{:S(2)}, u32[]{:S(2)}) %collective-permute-start.13) | collective-permute-done | bytes 180256 | tf_op jit(solution)/shard_map/ppermute | solution.py:511
  64.9 1.5 %maxima.3 = f32[128,128]{1,0:T(8,128)} custom-call(s32[44,128]{1,0:T(8,128)S(1)} %get-tuple-element.174.table_ref, f32[352,128]{1,0:T(8,128)S(1)} %get-tuple-element.175.p0, f32[352,128]{1,0:T(8,128)S(1)} %collective-permute-done.11.p1, f32[352,128]{1,0:T(8,128)S(1)} %collective-permute-done.12.p2, f32[352,128]{1,0:T(8,128)S(1)} %collective-permute-done.13.p3, ...), custom_call_target="tpu_custom_call" | custom-call | tf_op jit(solution)/shard_map/maxima/pallas_call | solution.py:519
  66.4 5.5 %all-to-all-start.8 = ((f32[128,1,128]{2,1,0:T(1,128)}), f32[128,1,128]{2,1,0:T(1,128)S(1)}, u32[]{:S(2)}, u32[]{:S(2)}) async-start(f32[128,1,128]{2,1,0:T(1,128)} %bitcast.17), calls=%async_computation.8 | async-start | bytes 131072 | tf_op jit(solution)/shard_map/all_to_all | solution.py:524
  71.8 9.5 %all-to-all-done.8 = f32[128,1,128]{2,1,0:T(1,128)S(1)} async-done(((f32[128,1,128]{2,1,0:T(1,128)}), f32[128,1,128]{2,1,0:T(1,128)S(1)}, u32[]{:S(2)}, u32[]{:S(2)}) %all-to-all-start.8) | async-done | bytes 65568 | tf_op jit(solution)/shard_map/all_to_all | solution.py:524
  81.3 0.6 pick.3
  (1 shorter events, 0.0 us)
Async XLA Ops:
  0.0 3.5 %copy-start.1 = (f32[128,4096]{1,0:T(8,128)S(1)}, f32[128,4096]{1,0:T(8,128)}, u32[]{:S(2)}) copy-start(f32[128,4096]{1,0:T(8,128)} %x_ref.3) | copy-start | bytes 6291460
  0.0 3.5 %copy-start = (s32[128]{0:T(128)S(1)}, s32[128]{0:T(128)}, u32[]{:S(2)}) copy-start(s32[128]{0:T(128)} %param.9) | copy-start | bytes 1540
  2.0 3.1 %collective-permute-start.7 = (bf16[144,2048]{1,0:T(8,128)(2,1)S(1)}, bf16[144,2048]{1,0:T(8,128)(2,1)S(1)}, u32[]{:S(2)}, u32[]{:S(2)}) collective-permute-start(bf16[144,2048]{1,0:T(8,128)(2,1)S(1)} %get-tuple-element.154), channel_id=1, source_target_pairs={{0,1},{1,0},{2,3},{3,2},{4,5},{5,4},{6,7},{7,6},{8,9},{9,8},{10,11... | collective-permute-start | bytes 1769480 | tf_op jit(solution)/shard_map/ppermute | solution.py:468
  40.9 3.2 %collective-permute-start.8 = (bf16[64,512]{1,0:T(8,128)(2,1)S(1)}, bf16[64,512]{1,0:T(8,128)(2,1)S(1)}, u32[]{:S(2)}, u32[]{:S(2)}) collective-permute-start(bf16[64,512]{1,0:T(8,128)(2,1)S(1)} %get-tuple-element.157), channel_id=1, source_target_pairs={{0,24},{8,0},{16,8},{24,16},{1,25},{9,1},{17,9},{25,17},{2,26},{10... | collective-permute-start | bytes 196616 | tf_op jit(solution)/shard_map/ppermute | solution.py:487
  44.2 6.5 %collective-permute-start.9 = (bf16[1216,512]{1,0:T(8,128)(2,1)S(1)}, bf16[1216,512]{1,0:T(8,128)(2,1)S(1)}, u32[]{:S(2)}, u32[]{:S(2)}) collective-permute-start(bf16[1216,512]{1,0:T(8,128)(2,1)S(1)} %get-tuple-element.161), channel_id=1, source_target_pairs={{0,1},{1,0},{2,3},{3,2},{4,5},{5,4},{6,7},{7,6},{8,9},{9,8},{10,11... | collective-permute-start | bytes 3735560 | tf_op jit(solution)/shard_map/ppermute | solution.py:494
  48.0 2.7 %collective-permute-start.10 = (bf16[64,512]{1,0:T(8,128)(2,1)S(1)}, bf16[64,512]{1,0:T(8,128)(2,1)S(1)}, u32[]{:S(2)}, u32[]{:S(2)}) collective-permute-start(bf16[64,512]{1,0:T(8,128)(2,1)S(1)} %collective-permute-done.8.guest_ref), channel_id=1, source_target_pairs={{0,1},{1,0},{2,3},{3,2},{4,5},{5,4},{6,7},{7,6},{8,9},{9,8},{10,11... | collective-permute-start | bytes 196616 | tf_op jit(solution)/shard_map/ppermute | solution.py:495
  52.3 6.1 %collective-permute-start.11 = (f32[352,128]{1,0:T(8,128)S(1)}, f32[352,128]{1,0:T(8,128)S(1)}, u32[]{:S(2)}, u32[]{:S(2)}) collective-permute-start(f32[352,128]{1,0:T(8,128)S(1)} %get-tuple-element.169), channel_id=1, source_target_pairs={{0,6},{2,0},{4,2},{6,4},{1,7},{3,1},{5,3},{7,5},{8,14},{10,8},{12,... | collective-permute-start | bytes 540680 | tf_op jit(solution)/shard_map/ppermute | solution.py:511
  53.1 7.2 %collective-permute-start.12 = (f32[352,128]{1,0:T(8,128)S(1)}, f32[352,128]{1,0:T(8,128)S(1)}, u32[]{:S(2)}, u32[]{:S(2)}) collective-permute-start(f32[352,128]{1,0:T(8,128)S(1)} %get-tuple-element.170), channel_id=1, source_target_pairs={{0,4},{2,6},{4,0},{6,2},{1,5},{3,7},{5,1},{7,3},{8,12},{10,14},{12... | collective-permute-start | bytes 540680 | tf_op jit(solution)/shard_map/ppermute | solution.py:511
  54.4 10.5 %collective-permute-start.13 = (f32[352,128]{1,0:T(8,128)S(1)}, f32[352,128]{1,0:T(8,128)S(1)}, u32[]{:S(2)}, u32[]{:S(2)}) collective-permute-start(f32[352,128]{1,0:T(8,128)S(1)} %get-tuple-element.171), channel_id=1, source_target_pairs={{0,2},{2,4},{4,6},{6,0},{1,3},{3,5},{5,7},{7,1},{8,10},{10,12},{12... | collective-permute-start | bytes 540680 | tf_op jit(solution)/shard_map/ppermute | solution.py:511
  66.4 14.9 %all-to-all-start.8 = ((f32[128,1,128]{2,1,0:T(1,128)}), f32[128,1,128]{2,1,0:T(1,128)S(1)}, u32[]{:S(2)}, u32[]{:S(2)}) async-start(f32[128,1,128]{2,1,0:T(1,128)} %bitcast.17), calls=%async_computation.8 | async-start | bytes 131072 | tf_op jit(solution)/shard_map/all_to_all | solution.py:524

commit v4 on v3

--- a/solution.py
+++ b/solution.py
@@ -508,7 +508,7 @@
         compiler_params=params(16), name="gram",
     )(meta, other, swapped, far, raw)
     arrived = [partial[0]] + [
-        lax.ppermute(partial[s], "y", [(i, (i + s) % 4) for i in range(4)]) for s in (3, 2, 1)
+        lax.ppermute(partial[s], "y", [(i, (i + s) % 4) for i in range(4)]) for s in (2, 1, 3)
     ]
     over, table = pl.pallas_call(
         functools.partial(fit_kernel, block, units),

time: 82.1 us -> 81 us (0.987)
  waiting for transfers between devices: 20.7 us -> 18.3 us
  starting transfers between devices: 13 us -> 14.3 us
    ppermute x3, waiting for transfers between devices: 8.74 us -> 6.34 us  [route(): lax.ppermute(partial[s], 'y', [(i, (i + s) % 4) for i in range(4)])]
    ppermute x3, starting transfers between devices: 2.15 us -> 3.84 us  [route(): lax.ppermute(partial[s], 'y', [(i, (i + s) % 4) for i in range(4)])]
  transfers between devices with their start and end apart: 8 -> 8, of which waited for: 6 -> 5; matrix products, arithmetic and copies ran while one was open for 1% -> 1% of each run, Pallas kernels for 7% -> 7%
where the time goes in v4:
time: 81 us; the launch traced here: 80.8 us
  blocking collectives  33.4 us (41%)
  waiting for transfers between devices  18.3 us (23%)
  starting transfers between devices  14.3 us (18%)
  Pallas kernels  13.5 us (17%)
    all_to_all x1, blocking collectives, route(): packed = lax.all_to_all(packed, ('x', 'z', 'y'), 0, 0, tiled=True)  33.4 us
    all_to_all x1, waiting for transfers between devices, route(): lax.all_to_all(best.reshape(2 * CHIPS, 1, LANES), ('c', 'x', 'z', 'y'), 0...  9.47 us
    ppermute x3, waiting for transfers between devices, route(): lax.ppermute(partial[s], 'y', [(i, (i + s) % 4) for i in range(4)])  6.34 us
    all_to_all x1, starting transfers between devices, route(): lax.all_to_all(best.reshape(2 * CHIPS, 1, LANES), ('c', 'x', 'z', 'y'), 0...  5.09 us
    ppermute x3, starting transfers between devices, route(): lax.ppermute(partial[s], 'y', [(i, (i + s) % 4) for i in range(4)])  3.84 us
    ppermute x1, starting transfers between devices, route(): other = lax.ppermute(send, 'c', [(0, 1), (1, 0)])  3.8 us
    pallas_call x1, Pallas kernels, route(): pl.pallas_call(functools.partial(sort_kernel, block), out_shape=(share, s...  3.15 us
    pallas_call x1, Pallas kernels, route(): pl.pallas_call(unit_send_kernel, out_shape=(half, shape((ROWS, LANES), f3...  1.98 us
  transfers between devices with their start and end apart: 8, of which 5 were waited for; matrix products, arithmetic and copies ran while one was open for 1% of the time, Pallas kernels for 7%

profile of v4, /device:TPU:1, one launch (start us, length us, event | category | flops | bytes accessed | tf_op | source)
XLA Modules:
  0.0 80.8 jit_solution(15108460152583295004)
XLA Ops:
  0.0 0.0 copy-start.1
  0.0 0.0 copy-start
  0.0 2.0 %unit_send.3 = (bf16[144,2048]{1,0:T(8,128)(2,1)S(1)}, f32[128,128]{1,0:T(8,128)S(1)}) custom-call(f32[128,4096]{1,0:T(8,128)} %x_ref.3, s32[1,128]{1,0:T(1,128)} %bitcast.35), custom_call_target="tpu_custom_call" | custom-call | tf_op jit(solution)/shard_map/unit_send/pallas_call | solution.py:464
  2.0 1.5 %collective-permute-start.7 = (bf16[144,2048]{1,0:T(8,128)(2,1)S(1)}, bf16[144,2048]{1,0:T(8,128)(2,1)S(1)}, u32[]{:S(2)}, u32[]{:S(2)}) collective-permute-start(bf16[144,2048]{1,0:T(8,128)(2,1)S(1)} %get-tuple-element.154), channel_id=1, source_target_pairs={{0,1},{1,0},{2,3},{3,2},{4,5},{5,4},{6,7},{7,6},{8,9},{9,8},{10,11... | collective-permute-start | bytes 1769480 | tf_op jit(solution)/shard_map/ppermute | solution.py:468
  3.5 0.0 copy-done.1
  3.5 0.0 copy-done
  3.5 0.2 unit_keep.3.keep_ref
  3.7 1.4 %collective-permute-done.7.got_ref = bf16[144,2048]{1,0:T(8,128)(2,1)S(1)} collective-permute-done((bf16[144,2048]{1,0:T(8,128)(2,1)S(1)}, bf16[144,2048]{1,0:T(8,128)(2,1)S(1)}, u32[]{:S(2)}, u32[]{:S(2)}) %collective-permute-start.7) | collective-permute-done | bytes 589856 | tf_op jit(solution)/shard_map/ppermute | solution.py:468
  5.1 0.8 %pack.3 = (bf16[64,24,512]{2,1,0:T(8,128)(2,1)S(1)}, s32[8,128]{1,0:T(8,128)S(1)}) custom-call(bf16[144,2048]{1,0:T(8,128)(2,1)S(1)} %unit_keep.3.keep_ref, bf16[144,2048]{1,0:T(8,128)(2,1)S(1)} %collective-permute-done.7.got_ref), custom_call_target="tpu_custom_call" | custom-call | tf_op jit(solution)/shard_map/pack/pallas_call | solution.py:475
  6.0 33.4 %all_to_all.61.x_ref = bf16[64,24,512]{2,1,0:T(8,128)(2,1)S(1)} all-to-all(bf16[64,24,512]{2,1,0:T(8,128)(2,1)S(1)} %get-tuple-element.155), channel_id=1, replica_groups=mesh['x'=4,'z'=4,'y'=4,'c'=2] {'x','z','y'}, dimensions={0} | all-to-all | bytes 3145728 | tf_op jit(solution)/shard_map/all_to_all | solution.py:480
  39.4 1.5 %names.3 = (bf16[64,512]{1,0:T(8,128)(2,1)S(1)}, s32[8,1536]{1,0:T(8,128)S(1)}, s32[64,128]{1,0:T(8,128)S(1)}, s32[64,128]{1,0:T(8,128)S(1)}, s32[8,128]{1,0:T(8,128)S(1)}) custom-call(bf16[64,24,512]{2,1,0:T(8,128)(2,1)S(1)} %all_to_all.61.x_ref), custom_call_target="tpu_custom_call" | custom-call | tf_op jit(solution)/shard_map/names/pallas_call | solution.py:482
  40.9 0.1 collective-permute-start.8
  41.0 3.1 %sort.3 = (bf16[1216,512]{1,0:T(8,128)(2,1)S(1)}, bf16[1216,512]{1,0:T(8,128)(2,1)S(1)}) custom-call(bf16[64,24,512]{2,1,0:T(8,128)(2,1)S(1)} %all_to_all.61.x_ref, s32[8,1536]{1,0:T(8,128)S(1)} %get-tuple-element.158.line_ref), custom_call_target="tpu_custom_call" | custom-call | tf_op jit(solution)/shard_map/sort/pallas_call | solution.py:489
  44.1 0.0 collective-permute-done.8.guest_ref
  44.2 3.8 %collective-permute-start.9 = (bf16[1216,512]{1,0:T(8,128)(2,1)S(1)}, bf16[1216,512]{1,0:T(8,128)(2,1)S(1)}, u32[]{:S(2)}, u32[]{:S(2)}) collective-permute-start(bf16[1216,512]{1,0:T(8,128)(2,1)S(1)} %get-tuple-element.161), channel_id=1, source_target_pairs={{0,1},{1,0},{2,3},{3,2},{4,5},{5,4},{6,7},{7,6},{8,9},{9,8},{10,11... | collective-permute-start | bytes 3735560 | tf_op jit(solution)/shard_map/ppermute | solution.py:494
  48.0 0.0 collective-permute-start.10
  48.0 1.6 %own.3 = (f32[2496,128]{1,0:T(8,128)S(1)}, s32[8,64]{1,0:T(8,128)S(1)}) custom-call(bf16[1216,512]{1,0:T(8,128)(2,1)S(1)} %get-tuple-element.163.x_ref, bf16[64,512]{1,0:T(8,128)(2,1)S(1)} %collective-permute-done.8.guest_ref, s32[64,128]{1,0:T(8,128)S(1)} %get-tuple-element.164.key_ref, s32[64,128]{1,0:T(8,128)S(1)} %get-tuple-element.165.pos_ref), custom_call_target="tpu_custom_call" | custom-call | flops 327155712 | bytes 4194304 | tf_op jit(solution)/shard_map/own/pallas_call | solution.py:496
  49.5 1.1 %collective-permute-done.10.guest_ref = bf16[64,512]{1,0:T(8,128)(2,1)S(1)} collective-permute-done((bf16[64,512]{1,0:T(8,128)(2,1)S(1)}, bf16[64,512]{1,0:T(8,128)(2,1)S(1)}, u32[]{:S(2)}, u32[]{:S(2)}) %collective-permute-start.10) | collective-permute-done | bytes 65568 | tf_op jit(solution)/shard_map/ppermute | solution.py:495
  50.6 0.0 collective-permute-done.9.x_ref
  50.6 1.6 %gram.3 = (f32[352,128]{1,0:T(8,128)S(1)}, f32[352,128]{1,0:T(8,128)S(1)}, f32[352,128]{1,0:T(8,128)S(1)}, f32[352,128]{1,0:T(8,128)S(1)}) custom-call(s32[8,128]{1,0:T(8,128)S(1)} %get-tuple-element.156.meta_ref, bf16[1216,512]{1,0:T(8,128)(2,1)S(1)} %collective-permute-done.9.x_ref, bf16[64,512]{1,0:T(8,128)(2,1)S(1)} %collective-permute-done.10.guest_ref, ...), custom_call_target="tpu_custom_call" | custom-call | tf_op jit(solution)/shard_map/gram/pallas_call | solution.py:503
  52.3 1.2 %collective-permute-start.11 = (f32[352,128]{1,0:T(8,128)S(1)}, f32[352,128]{1,0:T(8,128)S(1)}, u32[]{:S(2)}, u32[]{:S(2)}) collective-permute-start(f32[352,128]{1,0:T(8,128)S(1)} %get-tuple-element.169), channel_id=1, source_target_pairs={{0,4},{2,6},{4,0},{6,2},{1,5},{3,7},{5,1},{7,3},{8,12},{10,14},{12... | collective-permute-start | bytes 540680 | tf_op jit(solution)/shard_map/ppermute | solution.py:511
  53.4 0.2 collective-permute-start.12
  53.6 2.4 %collective-permute-start.13 = (f32[352,128]{1,0:T(8,128)S(1)}, f32[352,128]{1,0:T(8,128)S(1)}, u32[]{:S(2)}, u32[]{:S(2)}) collective-permute-start(f32[352,128]{1,0:T(8,128)S(1)} %get-tuple-element.171), channel_id=1, source_target_pairs={{0,6},{2,0},{4,2},{6,4},{1,7},{3,1},{5,3},{7,5},{8,14},{10,8},{12,... | collective-permute-start | bytes 540680 | tf_op jit(solution)/shard_map/ppermute | solution.py:511
  56.1 0.6 fit.3
  56.7 0.5 slice.6
  57.8 2.0 %collective-permute-done.11.p1 = f32[352,128]{1,0:T(8,128)S(1)} collective-permute-done((f32[352,128]{1,0:T(8,128)S(1)}, f32[352,128]{1,0:T(8,128)S(1)}, u32[]{:S(2)}, u32[]{:S(2)}) %collective-permute-start.11) | collective-permute-done | bytes 180256 | tf_op jit(solution)/shard_map/ppermute | solution.py:511
  59.9 4.3 %collective-permute-done.12.p2 = f32[352,128]{1,0:T(8,128)S(1)} collective-permute-done((f32[352,128]{1,0:T(8,128)S(1)}, f32[352,128]{1,0:T(8,128)S(1)}, u32[]{:S(2)}, u32[]{:S(2)}) %collective-permute-start.12) | collective-permute-done | bytes 180256 | tf_op jit(solution)/shard_map/ppermute | solution.py:511
  64.2 0.0 collective-permute-done.13.p3
  64.2 1.5 %maxima.3 = f32[128,128]{1,0:T(8,128)} custom-call(s32[44,128]{1,0:T(8,128)S(1)} %get-tuple-element.174.table_ref, f32[352,128]{1,0:T(8,128)S(1)} %get-tuple-element.175.p0, f32[352,128]{1,0:T(8,128)S(1)} %collective-permute-done.11.p1, f32[352,128]{1,0:T(8,128)S(1)} %collective-permute-done.12.p2, f32[352,128]{1,0:T(8,128)S(1)} %collective-permute-done.13.p3, ...), custom_call_target="tpu_custom_call" | custom-call | tf_op jit(solution)/shard_map/maxima/pallas_call | solution.py:519
  65.6 5.1 %all-to-all-start.8 = ((f32[128,1,128]{2,1,0:T(1,128)}), f32[128,1,128]{2,1,0:T(1,128)S(1)}, u32[]{:S(2)}, u32[]{:S(2)}) async-start(f32[128,1,128]{2,1,0:T(1,128)} %bitcast.17), calls=%async_computation.8 | async-start | bytes 131072 | tf_op jit(solution)/shard_map/all_to_all | solution.py:524
  70.7 9.5 %all-to-all-done.8 = f32[128,1,128]{2,1,0:T(1,128)S(1)} async-done(((f32[128,1,128]{2,1,0:T(1,128)}), f32[128,1,128]{2,1,0:T(1,128)S(1)}, u32[]{:S(2)}, u32[]{:S(2)}) %all-to-all-start.8) | async-done | bytes 65568 | tf_op jit(solution)/shard_map/all_to_all | solution.py:524
  80.2 0.6 pick.3
  (1 shorter events, 0.0 us)
Async XLA Ops:
  0.0 3.5 %copy-start.1 = (f32[128,4096]{1,0:T(8,128)S(1)}, f32[128,4096]{1,0:T(8,128)}, u32[]{:S(2)}) copy-start(f32[128,4096]{1,0:T(8,128)} %x_ref.3) | copy-start | bytes 6291460
  0.0 3.5 %copy-start = (s32[128]{0:T(128)S(1)}, s32[128]{0:T(128)}, u32[]{:S(2)}) copy-start(s32[128]{0:T(128)} %param.9) | copy-start | bytes 1540
  2.0 3.1 %collective-permute-start.7 = (bf16[144,2048]{1,0:T(8,128)(2,1)S(1)}, bf16[144,2048]{1,0:T(8,128)(2,1)S(1)}, u32[]{:S(2)}, u32[]{:S(2)}) collective-permute-start(bf16[144,2048]{1,0:T(8,128)(2,1)S(1)} %get-tuple-element.154), channel_id=1, source_target_pairs={{0,1},{1,0},{2,3},{3,2},{4,5},{5,4},{6,7},{7,6},{8,9},{9,8},{10,11... | collective-permute-start | bytes 1769480 | tf_op jit(solution)/shard_map/ppermute | solution.py:468
  40.9 3.2 %collective-permute-start.8 = (bf16[64,512]{1,0:T(8,128)(2,1)S(1)}, bf16[64,512]{1,0:T(8,128)(2,1)S(1)}, u32[]{:S(2)}, u32[]{:S(2)}) collective-permute-start(bf16[64,512]{1,0:T(8,128)(2,1)S(1)} %get-tuple-element.157), channel_id=1, source_target_pairs={{0,24},{8,0},{16,8},{24,16},{1,25},{9,1},{17,9},{25,17},{2,26},{10... | collective-permute-start | bytes 196616 | tf_op jit(solution)/shard_map/ppermute | solution.py:487
  44.2 6.5 %collective-permute-start.9 = (bf16[1216,512]{1,0:T(8,128)(2,1)S(1)}, bf16[1216,512]{1,0:T(8,128)(2,1)S(1)}, u32[]{:S(2)}, u32[]{:S(2)}) collective-permute-start(bf16[1216,512]{1,0:T(8,128)(2,1)S(1)} %get-tuple-element.161), channel_id=1, source_target_pairs={{0,1},{1,0},{2,3},{3,2},{4,5},{5,4},{6,7},{7,6},{8,9},{9,8},{10,11... | collective-permute-start | bytes 3735560 | tf_op jit(solution)/shard_map/ppermute | solution.py:494
  48.0 2.7 %collective-permute-start.10 = (bf16[64,512]{1,0:T(8,128)(2,1)S(1)}, bf16[64,512]{1,0:T(8,128)(2,1)S(1)}, u32[]{:S(2)}, u32[]{:S(2)}) collective-permute-start(bf16[64,512]{1,0:T(8,128)(2,1)S(1)} %collective-permute-done.8.guest_ref), channel_id=1, source_target_pairs={{0,1},{1,0},{2,3},{3,2},{4,5},{5,4},{6,7},{7,6},{8,9},{9,8},{10,11... | collective-permute-start | bytes 196616 | tf_op jit(solution)/shard_map/ppermute | solution.py:495
  52.3 7.6 %collective-permute-start.11 = (f32[352,128]{1,0:T(8,128)S(1)}, f32[352,128]{1,0:T(8,128)S(1)}, u32[]{:S(2)}, u32[]{:S(2)}) collective-permute-start(f32[352,128]{1,0:T(8,128)S(1)} %get-tuple-element.169), channel_id=1, source_target_pairs={{0,4},{2,6},{4,0},{6,2},{1,5},{3,7},{5,1},{7,3},{8,12},{10,14},{12... | collective-permute-start | bytes 540680 | tf_op jit(solution)/shard_map/ppermute | solution.py:511
  53.4 10.8 %collective-permute-start.12 = (f32[352,128]{1,0:T(8,128)S(1)}, f32[352,128]{1,0:T(8,128)S(1)}, u32[]{:S(2)}, u32[]{:S(2)}) collective-permute-start(f32[352,128]{1,0:T(8,128)S(1)} %get-tuple-element.170), channel_id=1, source_target_pairs={{0,2},{2,4},{4,6},{6,0},{1,3},{3,5},{5,7},{7,1},{8,10},{10,12},{12... | collective-permute-start | bytes 540680 | tf_op jit(solution)/shard_map/ppermute | solution.py:511
  53.6 10.5 %collective-permute-start.13 = (f32[352,128]{1,0:T(8,128)S(1)}, f32[352,128]{1,0:T(8,128)S(1)}, u32[]{:S(2)}, u32[]{:S(2)}) collective-permute-start(f32[352,128]{1,0:T(8,128)S(1)} %get-tuple-element.171), channel_id=1, source_target_pairs={{0,6},{2,0},{4,2},{6,4},{1,7},{3,1},{5,3},{7,5},{8,14},{10,8},{12,... | collective-permute-start | bytes 540680 | tf_op jit(solution)/shard_map/ppermute | solution.py:511
  65.6 14.6 %all-to-all-start.8 = ((f32[128,1,128]{2,1,0:T(1,128)}), f32[128,1,128]{2,1,0:T(1,128)S(1)}, u32[]{:S(2)}, u32[]{:S(2)}) async-start(f32[128,1,128]{2,1,0:T(1,128)} %bitcast.17), calls=%async_computation.8 | async-start | bytes 131072 | tf_op jit(solution)/shard_map/all_to_all | solution.py:524

commit v5 on v4

--- a/solution.py
+++ b/solution.py
@@ -297,6 +297,9 @@
 
 def add_guests(core, base_ref, guest_ref, far_ref, out_ref):
     guests, far = guest_ref[...], far_ref[:1, :]
+    filled = max(segment[2 + core] + segment[1] for segment in SEGMENTS if segment[2 + core] is not None)
+    if filled < SHARE_ROWS:
+        out_ref[filled:, :] = jnp.zeros((SHARE_ROWS - filled, WIDTH), bf16)
     for segment in SEGMENTS:
         at, rows = segment[2 + core], segment[1]
         if at is not None:
@@ -312,7 +315,7 @@
 RAW_ROWS = max(sum(CAPS[q] - first for q, first in share) for share in SHARES)
 
 
-def own_kernel(x_ref, guest_ref, key_ref, pos_ref, raw_ref, far_ref, rows_ref):
+def own_kernel(meta_ref, x_ref, guest_ref, key_ref, pos_ref, raw_ref, far_ref, rows_ref):
     total = jnp.zeros((8, GUESTS), f32)
     step = 16
     for first in range(0, CHIPS, step):
@@ -328,7 +331,10 @@
             at = 0
             for q, first, left, right in blocks_of(core):
                 rows = CAPS[q] - first
-                raw_ref[at:at + rows, :] = dot_last(rows_ref[left, :], rows_ref[right, :])
+                score = dot_last(rows_ref[left, :], rows_ref[right, :])
+                size = size_of(meta_ref, q) - first
+                i, j = iota(score.shape, 0), iota(score.shape, 1)
+                raw_ref[at:at + rows, :] = jnp.where((i < size) & (j < size) & (i != j), score, -4.0)
                 at += rows
 
 
@@ -360,12 +366,9 @@
                 rows = CAPS[q] - first
                 score = raw_ref[at:at + rows, :] + dot_last(rows_ref[left, :], rows_ref[right, :])
                 at += rows
-                size = size_of(meta_ref, q)
-                i, j = iota(score.shape, 0), iota(score.shape, 1)
-                keep = (i < size - first) & (j < size - first) & (i != j)
-                score = folded(jnp.where(keep, score, -4.0))
+                score = folded(score)
                 part_ref[pl.ds(pl.multiple_of(to, UNIT), score.shape[0]), :] = score
-                to = jnp.minimum(to + UNIT * length_of(size, first), 4 * units * UNIT)
+                to = jnp.minimum(to + UNIT * length_of(size_of(meta_ref, q), first), 4 * units * UNIT)
     chunk = units * UNIT
     for shift, out in enumerate((out0, out1, out2, out3)):
         out[...] = part_ref[pl.ds(pl.multiple_of(lax.rem(y + shift, 4) * chunk, UNIT), chunk), :]
@@ -495,11 +498,11 @@
     swapped = lax.ppermute(brought, "c", [(0, 1), (1, 0)])
     raw, far = pl.pallas_call(
         own_kernel, out_shape=(shape((RAW_ROWS, LANES), f32), shape((8, GUESTS), i32)),
-        in_specs=[WHOLE] * 4, out_specs=(WHOLE,) * 2,
+        in_specs=[WHOLE] * 5, out_specs=(WHOLE,) * 2,
         scratch_shapes=[pltpu.VMEM((SHARE_ROWS, WIDTH), bf16)],
         compiler_params=params(16), name="own",
         cost_estimate=pl.CostEstimate(flops=2 * RAW_ROWS * LANES * WIDTH, bytes_accessed=4 << 20, transcendentals=0),
-    )(mine, brought, key, pos)
+    )(meta, mine, brought, key, pos)
     partial = pl.pallas_call(
         functools.partial(gram_kernel, units),
         out_shape=[shape((units * UNIT, LANES), f32)] * 4,

time: 81 us -> 81.1 us (level)
  no operation moved by 1% of the time
where the time goes in v5:
time: 81.1 us; the launch traced here: 80.9 us
  blocking collectives  33.4 us (41%)
  waiting for transfers between devices  18.3 us (23%)
  starting transfers between devices  14.3 us (18%)
  Pallas kernels  13.7 us (17%)
    all_to_all x1, blocking collectives, route(): packed = lax.all_to_all(packed, ('x', 'z', 'y'), 0, 0, tiled=True)  33.4 us
    all_to_all x1, waiting for transfers between devices, route(): lax.all_to_all(best.reshape(2 * CHIPS, 1, LANES), ('c', 'x', 'z', 'y'), 0...  9.47 us
    ppermute x3, waiting for transfers between devices, route(): lax.ppermute(partial[s], 'y', [(i, (i + s) % 4) for i in range(4)])  6.36 us
    all_to_all x1, starting transfers between devices, route(): lax.all_to_all(best.reshape(2 * CHIPS, 1, LANES), ('c', 'x', 'z', 'y'), 0...  5.08 us
    ppermute x3, starting transfers between devices, route(): lax.ppermute(partial[s], 'y', [(i, (i + s) % 4) for i in range(4)])  3.82 us
    ppermute x1, starting transfers between devices, route(): other = lax.ppermute(send, 'c', [(0, 1), (1, 0)])  3.8 us
    pallas_call x1, Pallas kernels, route(): pl.pallas_call(functools.partial(sort_kernel, block), out_shape=(share, s...  3.15 us
    pallas_call x1, Pallas kernels, route(): pl.pallas_call(unit_send_kernel, out_shape=(half, shape((ROWS, LANES), f3...  1.98 us
  transfers between devices with their start and end apart: 8, of which 5 were waited for; matrix products, arithmetic and copies ran while one was open for 1% of the time, Pallas kernels for 7%

profile of v5, /device:TPU:1, one launch (start us, length us, event | category | flops | bytes accessed | tf_op | source)
XLA Modules:
  0.0 80.9 jit_solution(16387383030976893810)
XLA Ops:
  0.0 0.0 copy-start.1
  0.0 0.0 copy-start
  0.0 2.0 %unit_send.3 = (bf16[144,2048]{1,0:T(8,128)(2,1)S(1)}, f32[128,128]{1,0:T(8,128)S(1)}) custom-call(f32[128,4096]{1,0:T(8,128)} %x_ref.3, s32[1,128]{1,0:T(1,128)} %bitcast.35), custom_call_target="tpu_custom_call" | custom-call | tf_op jit(solution)/shard_map/unit_send/pallas_call | solution.py:467
  2.0 1.5 %collective-permute-start.7 = (bf16[144,2048]{1,0:T(8,128)(2,1)S(1)}, bf16[144,2048]{1,0:T(8,128)(2,1)S(1)}, u32[]{:S(2)}, u32[]{:S(2)}) collective-permute-start(bf16[144,2048]{1,0:T(8,128)(2,1)S(1)} %get-tuple-element.154), channel_id=1, source_target_pairs={{0,1},{1,0},{2,3},{3,2},{4,5},{5,4},{6,7},{7,6},{8,9},{9,8},{10,11... | collective-permute-start | bytes 1769480 | tf_op jit(solution)/shard_map/ppermute | solution.py:471
  3.5 0.0 copy-done.1
  3.5 0.0 copy-done
  3.5 0.2 unit_keep.3.keep_ref
  3.7 1.4 %collective-permute-done.7.got_ref = bf16[144,2048]{1,0:T(8,128)(2,1)S(1)} collective-permute-done((bf16[144,2048]{1,0:T(8,128)(2,1)S(1)}, bf16[144,2048]{1,0:T(8,128)(2,1)S(1)}, u32[]{:S(2)}, u32[]{:S(2)}) %collective-permute-start.7) | collective-permute-done | bytes 589856 | tf_op jit(solution)/shard_map/ppermute | solution.py:471
  5.1 0.8 %pack.3 = (bf16[64,24,512]{2,1,0:T(8,128)(2,1)S(1)}, s32[8,128]{1,0:T(8,128)S(1)}) custom-call(bf16[144,2048]{1,0:T(8,128)(2,1)S(1)} %unit_keep.3.keep_ref, bf16[144,2048]{1,0:T(8,128)(2,1)S(1)} %collective-permute-done.7.got_ref), custom_call_target="tpu_custom_call" | custom-call | tf_op jit(solution)/shard_map/pack/pallas_call | solution.py:478
  6.0 33.4 %all_to_all.61.x_ref = bf16[64,24,512]{2,1,0:T(8,128)(2,1)S(1)} all-to-all(bf16[64,24,512]{2,1,0:T(8,128)(2,1)S(1)} %get-tuple-element.155), channel_id=1, replica_groups=mesh['x'=4,'z'=4,'y'=4,'c'=2] {'x','z','y'}, dimensions={0} | all-to-all | bytes 3145728 | tf_op jit(solution)/shard_map/all_to_all | solution.py:483
  39.4 1.5 %names.3 = (bf16[64,512]{1,0:T(8,128)(2,1)S(1)}, s32[8,1536]{1,0:T(8,128)S(1)}, s32[64,128]{1,0:T(8,128)S(1)}, s32[64,128]{1,0:T(8,128)S(1)}, s32[8,128]{1,0:T(8,128)S(1)}) custom-call(bf16[64,24,512]{2,1,0:T(8,128)(2,1)S(1)} %all_to_all.61.x_ref), custom_call_target="tpu_custom_call" | custom-call | tf_op jit(solution)/shard_map/names/pallas_call | solution.py:485
  40.9 0.1 collective-permute-start.8
  41.0 3.1 %sort.3 = (bf16[1216,512]{1,0:T(8,128)(2,1)S(1)}, bf16[1216,512]{1,0:T(8,128)(2,1)S(1)}) custom-call(bf16[64,24,512]{2,1,0:T(8,128)(2,1)S(1)} %all_to_all.61.x_ref, s32[8,1536]{1,0:T(8,128)S(1)} %get-tuple-element.158.line_ref), custom_call_target="tpu_custom_call" | custom-call | tf_op jit(solution)/shard_map/sort/pallas_call | solution.py:492
  44.1 0.0 collective-permute-done.8.guest_ref
  44.2 3.8 %collective-permute-start.9 = (bf16[1216,512]{1,0:T(8,128)(2,1)S(1)}, bf16[1216,512]{1,0:T(8,128)(2,1)S(1)}, u32[]{:S(2)}, u32[]{:S(2)}) collective-permute-start(bf16[1216,512]{1,0:T(8,128)(2,1)S(1)} %get-tuple-element.161), channel_id=1, source_target_pairs={{0,1},{1,0},{2,3},{3,2},{4,5},{5,4},{6,7},{7,6},{8,9},{9,8},{10,11... | collective-permute-start | bytes 3735560 | tf_op jit(solution)/shard_map/ppermute | solution.py:497
  48.0 0.0 collective-permute-start.10
  48.0 1.6 %own.3 = (f32[2496,128]{1,0:T(8,128)S(1)}, s32[8,64]{1,0:T(8,128)S(1)}) custom-call(s32[8,128]{1,0:T(8,128)S(1)} %get-tuple-element.156.meta_ref, bf16[1216,512]{1,0:T(8,128)(2,1)S(1)} %get-tuple-element.163.x_ref, bf16[64,512]{1,0:T(8,128)(2,1)S(1)} %collective-permute-done.8.guest_ref, s32[64,128]{1,0:T(8,128)S(1)} %get-tuple-element.164.key_ref, ...), custom_call_target="tpu_custom_call" | custom-call | flops 327155712 | bytes 4194304 | tf_op jit(solution)/shard_map/own/pallas_call | solution.py:499
  49.6 1.0 %collective-permute-done.10.guest_ref = bf16[64,512]{1,0:T(8,128)(2,1)S(1)} collective-permute-done((bf16[64,512]{1,0:T(8,128)(2,1)S(1)}, bf16[64,512]{1,0:T(8,128)(2,1)S(1)}, u32[]{:S(2)}, u32[]{:S(2)}) %collective-permute-start.10) | collective-permute-done | bytes 65568 | tf_op jit(solution)/shard_map/ppermute | solution.py:498
  50.6 0.0 collective-permute-done.9.x_ref
  50.6 1.8 %gram.3 = (f32[352,128]{1,0:T(8,128)S(1)}, f32[352,128]{1,0:T(8,128)S(1)}, f32[352,128]{1,0:T(8,128)S(1)}, f32[352,128]{1,0:T(8,128)S(1)}) custom-call(s32[8,128]{1,0:T(8,128)S(1)} %get-tuple-element.156.meta_ref, bf16[1216,512]{1,0:T(8,128)(2,1)S(1)} %collective-permute-done.9.x_ref, bf16[64,512]{1,0:T(8,128)(2,1)S(1)} %collective-permute-done.10.guest_ref, ...), custom_call_target="tpu_custom_call" | custom-call | tf_op jit(solution)/shard_map/gram/pallas_call | solution.py:506
  52.4 1.1 %collective-permute-start.11 = (f32[352,128]{1,0:T(8,128)S(1)}, f32[352,128]{1,0:T(8,128)S(1)}, u32[]{:S(2)}, u32[]{:S(2)}) collective-permute-start(f32[352,128]{1,0:T(8,128)S(1)} %get-tuple-element.169), channel_id=1, source_target_pairs={{0,4},{2,6},{4,0},{6,2},{1,5},{3,7},{5,1},{7,3},{8,12},{10,14},{12... | collective-permute-start | bytes 540680 | tf_op jit(solution)/shard_map/ppermute | solution.py:514
  53.5 0.2 collective-permute-start.12
  53.8 2.4 %collective-permute-start.13 = (f32[352,128]{1,0:T(8,128)S(1)}, f32[352,128]{1,0:T(8,128)S(1)}, u32[]{:S(2)}, u32[]{:S(2)}) collective-permute-start(f32[352,128]{1,0:T(8,128)S(1)} %get-tuple-element.171), channel_id=1, source_target_pairs={{0,6},{2,0},{4,2},{6,4},{1,7},{3,1},{5,3},{7,5},{8,14},{10,8},{12,... | collective-permute-start | bytes 540680 | tf_op jit(solution)/shard_map/ppermute | solution.py:514
  56.2 0.6 fit.3
  56.8 0.5 slice.6
  57.9 2.1 %collective-permute-done.11.p1 = f32[352,128]{1,0:T(8,128)S(1)} collective-permute-done((f32[352,128]{1,0:T(8,128)S(1)}, f32[352,128]{1,0:T(8,128)S(1)}, u32[]{:S(2)}, u32[]{:S(2)}) %collective-permute-start.11) | collective-permute-done | bytes 180256 | tf_op jit(solution)/shard_map/ppermute | solution.py:514
  60.0 4.3 %collective-permute-done.12.p2 = f32[352,128]{1,0:T(8,128)S(1)} collective-permute-done((f32[352,128]{1,0:T(8,128)S(1)}, f32[352,128]{1,0:T(8,128)S(1)}, u32[]{:S(2)}, u32[]{:S(2)}) %collective-permute-start.12) | collective-permute-done | bytes 180256 | tf_op jit(solution)/shard_map/ppermute | solution.py:514
  64.3 0.0 collective-permute-done.13.p3
  64.3 1.5 %maxima.3 = f32[128,128]{1,0:T(8,128)} custom-call(s32[44,128]{1,0:T(8,128)S(1)} %get-tuple-element.174.table_ref, f32[352,128]{1,0:T(8,128)S(1)} %get-tuple-element.175.p0, f32[352,128]{1,0:T(8,128)S(1)} %collective-permute-done.11.p1, f32[352,128]{1,0:T(8,128)S(1)} %collective-permute-done.12.p2, f32[352,128]{1,0:T(8,128)S(1)} %collective-permute-done.13.p3, ...), custom_call_target="tpu_custom_call" | custom-call | tf_op jit(solution)/shard_map/maxima/pallas_call | solution.py:522
  65.8 5.1 %all-to-all-start.8 = ((f32[128,1,128]{2,1,0:T(1,128)}), f32[128,1,128]{2,1,0:T(1,128)S(1)}, u32[]{:S(2)}, u32[]{:S(2)}) async-start(f32[128,1,128]{2,1,0:T(1,128)} %bitcast.17), calls=%async_computation.8 | async-start | bytes 131072 | tf_op jit(solution)/shard_map/all_to_all | solution.py:527
  70.8 9.5 %all-to-all-done.8 = f32[128,1,128]{2,1,0:T(1,128)S(1)} async-done(((f32[128,1,128]{2,1,0:T(1,128)}), f32[128,1,128]{2,1,0:T(1,128)S(1)}, u32[]{:S(2)}, u32[]{:S(2)}) %all-to-all-start.8) | async-done | bytes 65568 | tf_op jit(solution)/shard_map/all_to_all | solution.py:527
  80.3 0.6 pick.3
  (1 shorter events, 0.0 us)
Async XLA Ops:
  0.0 3.5 %copy-start.1 = (f32[128,4096]{1,0:T(8,128)S(1)}, f32[128,4096]{1,0:T(8,128)}, u32[]{:S(2)}) copy-start(f32[128,4096]{1,0:T(8,128)} %x_ref.3) | copy-start | bytes 6291460
  0.0 3.5 %copy-start = (s32[128]{0:T(128)S(1)}, s32[128]{0:T(128)}, u32[]{:S(2)}) copy-start(s32[128]{0:T(128)} %param.9) | copy-start | bytes 1540
  2.0 3.1 %collective-permute-start.7 = (bf16[144,2048]{1,0:T(8,128)(2,1)S(1)}, bf16[144,2048]{1,0:T(8,128)(2,1)S(1)}, u32[]{:S(2)}, u32[]{:S(2)}) collective-permute-start(bf16[144,2048]{1,0:T(8,128)(2,1)S(1)} %get-tuple-element.154), channel_id=1, source_target_pairs={{0,1},{1,0},{2,3},{3,2},{4,5},{5,4},{6,7},{7,6},{8,9},{9,8},{10,11... | collective-permute-start | bytes 1769480 | tf_op jit(solution)/shard_map/ppermute | solution.py:471
  40.9 3.2 %collective-permute-start.8 = (bf16[64,512]{1,0:T(8,128)(2,1)S(1)}, bf16[64,512]{1,0:T(8,128)(2,1)S(1)}, u32[]{:S(2)}, u32[]{:S(2)}) collective-permute-start(bf16[64,512]{1,0:T(8,128)(2,1)S(1)} %get-tuple-element.157), channel_id=1, source_target_pairs={{0,24},{8,0},{16,8},{24,16},{1,25},{9,1},{17,9},{25,17},{2,26},{10... | collective-permute-start | bytes 196616 | tf_op jit(solution)/shard_map/ppermute | solution.py:490
  44.2 6.5 %collective-permute-start.9 = (bf16[1216,512]{1,0:T(8,128)(2,1)S(1)}, bf16[1216,512]{1,0:T(8,128)(2,1)S(1)}, u32[]{:S(2)}, u32[]{:S(2)}) collective-permute-start(bf16[1216,512]{1,0:T(8,128)(2,1)S(1)} %get-tuple-element.161), channel_id=1, source_target_pairs={{0,1},{1,0},{2,3},{3,2},{4,5},{5,4},{6,7},{7,6},{8,9},{9,8},{10,11... | collective-permute-start | bytes 3735560 | tf_op jit(solution)/shard_map/ppermute | solution.py:497
  48.0 2.7 %collective-permute-start.10 = (bf16[64,512]{1,0:T(8,128)(2,1)S(1)}, bf16[64,512]{1,0:T(8,128)(2,1)S(1)}, u32[]{:S(2)}, u32[]{:S(2)}) collective-permute-start(bf16[64,512]{1,0:T(8,128)(2,1)S(1)} %collective-permute-done.8.guest_ref), channel_id=1, source_target_pairs={{0,1},{1,0},{2,3},{3,2},{4,5},{5,4},{6,7},{7,6},{8,9},{9,8},{10,11... | collective-permute-start | bytes 196616 | tf_op jit(solution)/shard_map/ppermute | solution.py:498
  52.4 7.6 %collective-permute-start.11 = (f32[352,128]{1,0:T(8,128)S(1)}, f32[352,128]{1,0:T(8,128)S(1)}, u32[]{:S(2)}, u32[]{:S(2)}) collective-permute-start(f32[352,128]{1,0:T(8,128)S(1)} %get-tuple-element.169), channel_id=1, source_target_pairs={{0,4},{2,6},{4,0},{6,2},{1,5},{3,7},{5,1},{7,3},{8,12},{10,14},{12... | collective-permute-start | bytes 540680 | tf_op jit(solution)/shard_map/ppermute | solution.py:514
  53.5 10.8 %collective-permute-start.12 = (f32[352,128]{1,0:T(8,128)S(1)}, f32[352,128]{1,0:T(8,128)S(1)}, u32[]{:S(2)}, u32[]{:S(2)}) collective-permute-start(f32[352,128]{1,0:T(8,128)S(1)} %get-tuple-element.170), channel_id=1, source_target_pairs={{0,2},{2,4},{4,6},{6,0},{1,3},{3,5},{5,7},{7,1},{8,10},{10,12},{12... | collective-permute-start | bytes 540680 | tf_op jit(solution)/shard_map/ppermute | solution.py:514
  53.8 10.5 %collective-permute-start.13 = (f32[352,128]{1,0:T(8,128)S(1)}, f32[352,128]{1,0:T(8,128)S(1)}, u32[]{:S(2)}, u32[]{:S(2)}) collective-permute-start(f32[352,128]{1,0:T(8,128)S(1)} %get-tuple-element.171), channel_id=1, source_target_pairs={{0,6},{2,0},{4,2},{6,4},{1,7},{3,1},{5,3},{7,5},{8,14},{10,8},{12,... | collective-permute-start | bytes 540680 | tf_op jit(solution)/shard_map/ppermute | solution.py:514
  65.8 14.6 %all-to-all-start.8 = ((f32[128,1,128]{2,1,0:T(1,128)}), f32[128,1,128]{2,1,0:T(1,128)S(1)}, u32[]{:S(2)}, u32[]{:S(2)}) async-start(f32[128,1,128]{2,1,0:T(1,128)} %bitcast.17), calls=%async_computation.8 | async-start | bytes 131072 | tf_op jit(solution)/shard_map/all_to_all | solution.py:527

commit v6 on v4

--- a/solution.py
+++ b/solution.py
@@ -196,6 +196,10 @@
         n.append(jnp.sum(size, axis=1, keepdims=True))
     wide = lambda v: jnp.broadcast_to(v, (1, LANES))
     meta_ref[...] = jnp.concatenate([wide(v) for v in in_order(n)] * 2, axis=0).astype(i32)
+    guest = valid & (home != group)
+    guest16, members16 = as_bf16(guest), [as_bf16(member) for member in members]
+    along = dot(jnp.concatenate(members16, axis=0), upper)
+    earlier = dot(lower, jnp.concatenate(members16 + [guest16], axis=1))
     pos = jnp.full(labels.shape, -1.0, f32)
     for r, member in enumerate(members):
         place = sum(
@@ -205,15 +209,13 @@
             place < 0.5, float(STARTS[0]),
             jnp.where(place < 1.5, float(STARTS[1]), jnp.where(place < 2.5, float(STARTS[2]), float(STARTS[3]))),
         )
-        member16 = as_bf16(member)
-        rank = dot(member16, upper) + jnp.sum(dot(lower, member16), axis=1, keepdims=True)
+        rank = along[CHIPS * r:CHIPS * (r + 1)] + jnp.sum(
+            earlier[:, LANES * r:LANES * (r + 1)], axis=1, keepdims=True)
         pos = jnp.where(member, start + rank, pos)
     pos = pos.astype(i32)
     pos_ref[...] = pos
-    guest = valid & (home != group)
-    guest16 = as_bf16(guest)
     same = (row >> 5) == (col >> 5)
-    turn = dot(guest16, as_bf16(same & (row < col))) + dot(dot(lower, guest16).astype(bf16), as_bf16(same))
+    turn = dot(guest16, as_bf16(same & (row < col))) + dot(earlier[:, 4 * LANES:].astype(bf16), as_bf16(same))
     turn = turn.astype(i32)
     away = at_home & (group != z) & (turn < GUESTS)
     key_ref[...] = jnp.where(away, turn, -1)

time: 81 us -> 81 us (level)
  no operation moved by 1% of the time
where the time goes in v6:
time: 81 us; the launch traced here: 80.8 us
  blocking collectives  33.4 us (41%)
  waiting for transfers between devices  18.3 us (23%)
  starting transfers between devices  14.3 us (18%)
  Pallas kernels  13.5 us (17%)
    all_to_all x1, blocking collectives, route(): packed = lax.all_to_all(packed, ('x', 'z', 'y'), 0, 0, tiled=True)  33.4 us
    all_to_all x1, waiting for transfers between devices, route(): lax.all_to_all(best.reshape(2 * CHIPS, 1, LANES), ('c', 'x', 'z', 'y'), 0...  9.47 us
    ppermute x3, waiting for transfers between devices, route(): lax.ppermute(partial[s], 'y', [(i, (i + s) % 4) for i in range(4)])  6.34 us
    all_to_all x1, starting transfers between devices, route(): lax.all_to_all(best.reshape(2 * CHIPS, 1, LANES), ('c', 'x', 'z', 'y'), 0...  5.09 us
    ppermute x3, starting transfers between devices, route(): lax.ppermute(partial[s], 'y', [(i, (i + s) % 4) for i in range(4)])  3.84 us
    ppermute x1, starting transfers between devices, route(): other = lax.ppermute(send, 'c', [(0, 1), (1, 0)])  3.8 us
    pallas_call x1, Pallas kernels, route(): pl.pallas_call(functools.partial(sort_kernel, block), out_shape=(share, s...  3.15 us
    pallas_call x1, Pallas kernels, route(): pl.pallas_call(unit_send_kernel, out_shape=(half, shape((ROWS, LANES), f3...  1.98 us
  transfers between devices with their start and end apart: 8, of which 5 were waited for; matrix products, arithmetic and copies ran while one was open for 1% of the time, Pallas kernels for 7%

profile of v6, /device:TPU:1, one launch (start us, length us, event | category | flops | bytes accessed | tf_op | source)
XLA Modules:
  0.0 80.8 jit_solution(14734024010699350532)
XLA Ops:
  0.0 0.0 copy-start.1
  0.0 0.0 copy-start
  0.0 2.0 %unit_send.3 = (bf16[144,2048]{1,0:T(8,128)(2,1)S(1)}, f32[128,128]{1,0:T(8,128)S(1)}) custom-call(f32[128,4096]{1,0:T(8,128)} %x_ref.3, s32[1,128]{1,0:T(1,128)} %bitcast.35), custom_call_target="tpu_custom_call" | custom-call | tf_op jit(solution)/shard_map/unit_send/pallas_call | solution.py:466
  2.0 1.5 %collective-permute-start.7 = (bf16[144,2048]{1,0:T(8,128)(2,1)S(1)}, bf16[144,2048]{1,0:T(8,128)(2,1)S(1)}, u32[]{:S(2)}, u32[]{:S(2)}) collective-permute-start(bf16[144,2048]{1,0:T(8,128)(2,1)S(1)} %get-tuple-element.154), channel_id=1, source_target_pairs={{0,1},{1,0},{2,3},{3,2},{4,5},{5,4},{6,7},{7,6},{8,9},{9,8},{10,11... | collective-permute-start | bytes 1769480 | tf_op jit(solution)/shard_map/ppermute | solution.py:470
  3.5 0.0 copy-done.1
  3.5 0.0 copy-done
  3.5 0.2 unit_keep.3.keep_ref
  3.7 1.4 %collective-permute-done.7.got_ref = bf16[144,2048]{1,0:T(8,128)(2,1)S(1)} collective-permute-done((bf16[144,2048]{1,0:T(8,128)(2,1)S(1)}, bf16[144,2048]{1,0:T(8,128)(2,1)S(1)}, u32[]{:S(2)}, u32[]{:S(2)}) %collective-permute-start.7) | collective-permute-done | bytes 589856 | tf_op jit(solution)/shard_map/ppermute | solution.py:470
  5.1 0.8 %pack.3 = (bf16[64,24,512]{2,1,0:T(8,128)(2,1)S(1)}, s32[8,128]{1,0:T(8,128)S(1)}) custom-call(bf16[144,2048]{1,0:T(8,128)(2,1)S(1)} %unit_keep.3.keep_ref, bf16[144,2048]{1,0:T(8,128)(2,1)S(1)} %collective-permute-done.7.got_ref), custom_call_target="tpu_custom_call" | custom-call | tf_op jit(solution)/shard_map/pack/pallas_call | solution.py:477
  6.0 33.4 %all_to_all.61.x_ref = bf16[64,24,512]{2,1,0:T(8,128)(2,1)S(1)} all-to-all(bf16[64,24,512]{2,1,0:T(8,128)(2,1)S(1)} %get-tuple-element.155), channel_id=1, replica_groups=mesh['x'=4,'z'=4,'y'=4,'c'=2] {'x','z','y'}, dimensions={0} | all-to-all | bytes 3145728 | tf_op jit(solution)/shard_map/all_to_all | solution.py:482
  39.4 1.5 %names.3 = (bf16[64,512]{1,0:T(8,128)(2,1)S(1)}, s32[8,1536]{1,0:T(8,128)S(1)}, s32[64,128]{1,0:T(8,128)S(1)}, s32[64,128]{1,0:T(8,128)S(1)}, s32[8,128]{1,0:T(8,128)S(1)}) custom-call(bf16[64,24,512]{2,1,0:T(8,128)(2,1)S(1)} %all_to_all.61.x_ref), custom_call_target="tpu_custom_call" | custom-call | tf_op jit(solution)/shard_map/names/pallas_call | solution.py:484
  40.9 0.1 collective-permute-start.8
  41.0 3.1 %sort.3 = (bf16[1216,512]{1,0:T(8,128)(2,1)S(1)}, bf16[1216,512]{1,0:T(8,128)(2,1)S(1)}) custom-call(bf16[64,24,512]{2,1,0:T(8,128)(2,1)S(1)} %all_to_all.61.x_ref, s32[8,1536]{1,0:T(8,128)S(1)} %get-tuple-element.158.line_ref), custom_call_target="tpu_custom_call" | custom-call | tf_op jit(solution)/shard_map/sort/pallas_call | solution.py:491
  44.2 0.0 collective-permute-done.8.guest_ref
  44.2 3.8 %collective-permute-start.9 = (bf16[1216,512]{1,0:T(8,128)(2,1)S(1)}, bf16[1216,512]{1,0:T(8,128)(2,1)S(1)}, u32[]{:S(2)}, u32[]{:S(2)}) collective-permute-start(bf16[1216,512]{1,0:T(8,128)(2,1)S(1)} %get-tuple-element.161), channel_id=1, source_target_pairs={{0,1},{1,0},{2,3},{3,2},{4,5},{5,4},{6,7},{7,6},{8,9},{9,8},{10,11... | collective-permute-start | bytes 3735560 | tf_op jit(solution)/shard_map/ppermute | solution.py:496
  48.0 0.0 collective-permute-start.10
  48.0 1.6 %own.3 = (f32[2496,128]{1,0:T(8,128)S(1)}, s32[8,64]{1,0:T(8,128)S(1)}) custom-call(bf16[1216,512]{1,0:T(8,128)(2,1)S(1)} %get-tuple-element.163.x_ref, bf16[64,512]{1,0:T(8,128)(2,1)S(1)} %collective-permute-done.8.guest_ref, s32[64,128]{1,0:T(8,128)S(1)} %get-tuple-element.164.key_ref, s32[64,128]{1,0:T(8,128)S(1)} %get-tuple-element.165.pos_ref), custom_call_target="tpu_custom_call" | custom-call | flops 327155712 | bytes 4194304 | tf_op jit(solution)/shard_map/own/pallas_call | solution.py:498
  49.5 1.1 %collective-permute-done.10.guest_ref = bf16[64,512]{1,0:T(8,128)(2,1)S(1)} collective-permute-done((bf16[64,512]{1,0:T(8,128)(2,1)S(1)}, bf16[64,512]{1,0:T(8,128)(2,1)S(1)}, u32[]{:S(2)}, u32[]{:S(2)}) %collective-permute-start.10) | collective-permute-done | bytes 65568 | tf_op jit(solution)/shard_map/ppermute | solution.py:497
  50.6 0.0 collective-permute-done.9.x_ref
  50.6 1.6 %gram.3 = (f32[352,128]{1,0:T(8,128)S(1)}, f32[352,128]{1,0:T(8,128)S(1)}, f32[352,128]{1,0:T(8,128)S(1)}, f32[352,128]{1,0:T(8,128)S(1)}) custom-call(s32[8,128]{1,0:T(8,128)S(1)} %get-tuple-element.156.meta_ref, bf16[1216,512]{1,0:T(8,128)(2,1)S(1)} %collective-permute-done.9.x_ref, bf16[64,512]{1,0:T(8,128)(2,1)S(1)} %collective-permute-done.10.guest_ref, ...), custom_call_target="tpu_custom_call" | custom-call | tf_op jit(solution)/shard_map/gram/pallas_call | solution.py:505
  52.3 1.2 %collective-permute-start.11 = (f32[352,128]{1,0:T(8,128)S(1)}, f32[352,128]{1,0:T(8,128)S(1)}, u32[]{:S(2)}, u32[]{:S(2)}) collective-permute-start(f32[352,128]{1,0:T(8,128)S(1)} %get-tuple-element.169), channel_id=1, source_target_pairs={{0,4},{2,6},{4,0},{6,2},{1,5},{3,7},{5,1},{7,3},{8,12},{10,14},{12... | collective-permute-start | bytes 540680 | tf_op jit(solution)/shard_map/ppermute | solution.py:513
  53.4 0.2 collective-permute-start.12
  53.7 2.4 %collective-permute-start.13 = (f32[352,128]{1,0:T(8,128)S(1)}, f32[352,128]{1,0:T(8,128)S(1)}, u32[]{:S(2)}, u32[]{:S(2)}) collective-permute-start(f32[352,128]{1,0:T(8,128)S(1)} %get-tuple-element.171), channel_id=1, source_target_pairs={{0,6},{2,0},{4,2},{6,4},{1,7},{3,1},{5,3},{7,5},{8,14},{10,8},{12,... | collective-permute-start | bytes 540680 | tf_op jit(solution)/shard_map/ppermute | solution.py:513
  56.1 0.6 fit.3
  56.7 0.5 slice.6
  57.9 2.0 %collective-permute-done.11.p1 = f32[352,128]{1,0:T(8,128)S(1)} collective-permute-done((f32[352,128]{1,0:T(8,128)S(1)}, f32[352,128]{1,0:T(8,128)S(1)}, u32[]{:S(2)}, u32[]{:S(2)}) %collective-permute-start.11) | collective-permute-done | bytes 180256 | tf_op jit(solution)/shard_map/ppermute | solution.py:513
  59.9 4.3 %collective-permute-done.12.p2 = f32[352,128]{1,0:T(8,128)S(1)} collective-permute-done((f32[352,128]{1,0:T(8,128)S(1)}, f32[352,128]{1,0:T(8,128)S(1)}, u32[]{:S(2)}, u32[]{:S(2)}) %collective-permute-start.12) | collective-permute-done | bytes 180256 | tf_op jit(solution)/shard_map/ppermute | solution.py:513
  64.2 0.0 collective-permute-done.13.p3
  64.2 1.5 %maxima.3 = f32[128,128]{1,0:T(8,128)} custom-call(s32[44,128]{1,0:T(8,128)S(1)} %get-tuple-element.174.table_ref, f32[352,128]{1,0:T(8,128)S(1)} %get-tuple-element.175.p0, f32[352,128]{1,0:T(8,128)S(1)} %collective-permute-done.11.p1, f32[352,128]{1,0:T(8,128)S(1)} %collective-permute-done.12.p2, f32[352,128]{1,0:T(8,128)S(1)} %collective-permute-done.13.p3, ...), custom_call_target="tpu_custom_call" | custom-call | tf_op jit(solution)/shard_map/maxima/pallas_call | solution.py:521
  65.7 5.1 %all-to-all-start.8 = ((f32[128,1,128]{2,1,0:T(1,128)}), f32[128,1,128]{2,1,0:T(1,128)S(1)}, u32[]{:S(2)}, u32[]{:S(2)}) async-start(f32[128,1,128]{2,1,0:T(1,128)} %bitcast.17), calls=%async_computation.8 | async-start | bytes 131072 | tf_op jit(solution)/shard_map/all_to_all | solution.py:526
  70.8 9.5 %all-to-all-done.8 = f32[128,1,128]{2,1,0:T(1,128)S(1)} async-done(((f32[128,1,128]{2,1,0:T(1,128)}), f32[128,1,128]{2,1,0:T(1,128)S(1)}, u32[]{:S(2)}, u32[]{:S(2)}) %all-to-all-start.8) | async-done | bytes 65568 | tf_op jit(solution)/shard_map/all_to_all | solution.py:526
  80.2 0.6 pick.3
  (1 shorter events, 0.0 us)
Async XLA Ops:
  0.0 3.5 %copy-start.1 = (f32[128,4096]{1,0:T(8,128)S(1)}, f32[128,4096]{1,0:T(8,128)}, u32[]{:S(2)}) copy-start(f32[128,4096]{1,0:T(8,128)} %x_ref.3) | copy-start | bytes 6291460
  0.0 3.5 %copy-start = (s32[128]{0:T(128)S(1)}, s32[128]{0:T(128)}, u32[]{:S(2)}) copy-start(s32[128]{0:T(128)} %param.9) | copy-start | bytes 1540
  2.0 3.1 %collective-permute-start.7 = (bf16[144,2048]{1,0:T(8,128)(2,1)S(1)}, bf16[144,2048]{1,0:T(8,128)(2,1)S(1)}, u32[]{:S(2)}, u32[]{:S(2)}) collective-permute-start(bf16[144,2048]{1,0:T(8,128)(2,1)S(1)} %get-tuple-element.154), channel_id=1, source_target_pairs={{0,1},{1,0},{2,3},{3,2},{4,5},{5,4},{6,7},{7,6},{8,9},{9,8},{10,11... | collective-permute-start | bytes 1769480 | tf_op jit(solution)/shard_map/ppermute | solution.py:470
  40.9 3.2 %collective-permute-start.8 = (bf16[64,512]{1,0:T(8,128)(2,1)S(1)}, bf16[64,512]{1,0:T(8,128)(2,1)S(1)}, u32[]{:S(2)}, u32[]{:S(2)}) collective-permute-start(bf16[64,512]{1,0:T(8,128)(2,1)S(1)} %get-tuple-element.157), channel_id=1, source_target_pairs={{0,24},{8,0},{16,8},{24,16},{1,25},{9,1},{17,9},{25,17},{2,26},{10... | collective-permute-start | bytes 196616 | tf_op jit(solution)/shard_map/ppermute | solution.py:489
  44.2 6.5 %collective-permute-start.9 = (bf16[1216,512]{1,0:T(8,128)(2,1)S(1)}, bf16[1216,512]{1,0:T(8,128)(2,1)S(1)}, u32[]{:S(2)}, u32[]{:S(2)}) collective-permute-start(bf16[1216,512]{1,0:T(8,128)(2,1)S(1)} %get-tuple-element.161), channel_id=1, source_target_pairs={{0,1},{1,0},{2,3},{3,2},{4,5},{5,4},{6,7},{7,6},{8,9},{9,8},{10,11... | collective-permute-start | bytes 3735560 | tf_op jit(solution)/shard_map/ppermute | solution.py:496
  48.0 2.7 %collective-permute-start.10 = (bf16[64,512]{1,0:T(8,128)(2,1)S(1)}, bf16[64,512]{1,0:T(8,128)(2,1)S(1)}, u32[]{:S(2)}, u32[]{:S(2)}) collective-permute-start(bf16[64,512]{1,0:T(8,128)(2,1)S(1)} %collective-permute-done.8.guest_ref), channel_id=1, source_target_pairs={{0,1},{1,0},{2,3},{3,2},{4,5},{5,4},{6,7},{7,6},{8,9},{9,8},{10,11... | collective-permute-start | bytes 196616 | tf_op jit(solution)/shard_map/ppermute | solution.py:497
  52.3 7.6 %collective-permute-start.11 = (f32[352,128]{1,0:T(8,128)S(1)}, f32[352,128]{1,0:T(8,128)S(1)}, u32[]{:S(2)}, u32[]{:S(2)}) collective-permute-start(f32[352,128]{1,0:T(8,128)S(1)} %get-tuple-element.169), channel_id=1, source_target_pairs={{0,4},{2,6},{4,0},{6,2},{1,5},{3,7},{5,1},{7,3},{8,12},{10,14},{12... | collective-permute-start | bytes 540680 | tf_op jit(solution)/shard_map/ppermute | solution.py:513
  53.4 10.8 %collective-permute-start.12 = (f32[352,128]{1,0:T(8,128)S(1)}, f32[352,128]{1,0:T(8,128)S(1)}, u32[]{:S(2)}, u32[]{:S(2)}) collective-permute-start(f32[352,128]{1,0:T(8,128)S(1)} %get-tuple-element.170), channel_id=1, source_target_pairs={{0,2},{2,4},{4,6},{6,0},{1,3},{3,5},{5,7},{7,1},{8,10},{10,12},{12... | collective-permute-start | bytes 540680 | tf_op jit(solution)/shard_map/ppermute | solution.py:513
  53.7 10.5 %collective-permute-start.13 = (f32[352,128]{1,0:T(8,128)S(1)}, f32[352,128]{1,0:T(8,128)S(1)}, u32[]{:S(2)}, u32[]{:S(2)}) collective-permute-start(f32[352,128]{1,0:T(8,128)S(1)} %get-tuple-element.171), channel_id=1, source_target_pairs={{0,6},{2,0},{4,2},{6,4},{1,7},{3,1},{5,3},{7,5},{8,14},{10,8},{12,... | collective-permute-start | bytes 540680 | tf_op jit(solution)/shard_map/ppermute | solution.py:513
  65.7 14.6 %all-to-all-start.8 = ((f32[128,1,128]{2,1,0:T(1,128)}), f32[128,1,128]{2,1,0:T(1,128)S(1)}, u32[]{:S(2)}, u32[]{:S(2)}) async-start(f32[128,1,128]{2,1,0:T(1,128)} %bitcast.17), calls=%async_computation.8 | async-start | bytes 131072 | tf_op jit(solution)/shard_map/all_to_all | solution.py:526

commit v7 on v4

--- a/solution.py
+++ b/solution.py
@@ -350,7 +350,7 @@
 
 def gram_kernel(units, meta_ref, x_ref, guest_ref, far_ref, raw_ref, out0, out1, out2, out3, part_ref, rows_ref):
     y, c = index_on("y"), index_on("c")
-    part_ref[...] = jnp.full(part_ref.shape, -4.0, f32)
+    part_ref[:4 * units * UNIT, :] = jnp.full((4 * units * UNIT, LANES), -4.0, f32)
     for core in range(2):
         @pl.when(c == core)
         def _():

time: 81 us -> 81 us (level)
  no operation moved by 1% of the time
where the time goes in v7:
time: 81 us; the launch traced here: 80.8 us
  blocking collectives  33.4 us (41%)
  waiting for transfers between devices  18.3 us (23%)
  starting transfers between devices  14.3 us (18%)
  Pallas kernels  13.5 us (17%)
    all_to_all x1, blocking collectives, route(): packed = lax.all_to_all(packed, ('x', 'z', 'y'), 0, 0, tiled=True)  33.4 us
    all_to_all x1, waiting for transfers between devices, route(): lax.all_to_all(best.reshape(2 * CHIPS, 1, LANES), ('c', 'x', 'z', 'y'), 0...  9.47 us
    ppermute x3, waiting for transfers between devices, route(): lax.ppermute(partial[s], 'y', [(i, (i + s) % 4) for i in range(4)])  6.35 us
    all_to_all x1, starting transfers between devices, route(): lax.all_to_all(best.reshape(2 * CHIPS, 1, LANES), ('c', 'x', 'z', 'y'), 0...  5.09 us
    ppermute x3, starting transfers between devices, route(): lax.ppermute(partial[s], 'y', [(i, (i + s) % 4) for i in range(4)])  3.83 us
    ppermute x1, starting transfers between devices, route(): other = lax.ppermute(send, 'c', [(0, 1), (1, 0)])  3.8 us
    pallas_call x1, Pallas kernels, route(): pl.pallas_call(functools.partial(sort_kernel, block), out_shape=(share, s...  3.15 us
    pallas_call x1, Pallas kernels, route(): pl.pallas_call(unit_send_kernel, out_shape=(half, shape((ROWS, LANES), f3...  1.98 us
  transfers between devices with their start and end apart: 8, of which 5 were waited for; matrix products, arithmetic and copies ran while one was open for 1% of the time, Pallas kernels for 7%

profile of v7, /device:TPU:1, one launch (start us, length us, event | category | flops | bytes accessed | tf_op | source)
XLA Modules:
  0.0 80.8 jit_solution(11469446136630978563)
XLA Ops:
  0.0 0.0 copy-start.1
  0.0 0.0 copy-start
  0.0 2.0 %unit_send.3 = (bf16[144,2048]{1,0:T(8,128)(2,1)S(1)}, f32[128,128]{1,0:T(8,128)S(1)}) custom-call(f32[128,4096]{1,0:T(8,128)} %x_ref.3, s32[1,128]{1,0:T(1,128)} %bitcast.35), custom_call_target="tpu_custom_call" | custom-call | tf_op jit(solution)/shard_map/unit_send/pallas_call | solution.py:464
  2.0 1.5 %collective-permute-start.7 = (bf16[144,2048]{1,0:T(8,128)(2,1)S(1)}, bf16[144,2048]{1,0:T(8,128)(2,1)S(1)}, u32[]{:S(2)}, u32[]{:S(2)}) collective-permute-start(bf16[144,2048]{1,0:T(8,128)(2,1)S(1)} %get-tuple-element.154), channel_id=1, source_target_pairs={{0,1},{1,0},{2,3},{3,2},{4,5},{5,4},{6,7},{7,6},{8,9},{9,8},{10,11... | collective-permute-start | bytes 1769480 | tf_op jit(solution)/shard_map/ppermute | solution.py:468
  3.5 0.0 copy-done.1
  3.5 0.0 copy-done
  3.5 0.2 unit_keep.3.keep_ref
  3.7 1.4 %collective-permute-done.7.got_ref = bf16[144,2048]{1,0:T(8,128)(2,1)S(1)} collective-permute-done((bf16[144,2048]{1,0:T(8,128)(2,1)S(1)}, bf16[144,2048]{1,0:T(8,128)(2,1)S(1)}, u32[]{:S(2)}, u32[]{:S(2)}) %collective-permute-start.7) | collective-permute-done | bytes 589856 | tf_op jit(solution)/shard_map/ppermute | solution.py:468
  5.1 0.8 %pack.3 = (bf16[64,24,512]{2,1,0:T(8,128)(2,1)S(1)}, s32[8,128]{1,0:T(8,128)S(1)}) custom-call(bf16[144,2048]{1,0:T(8,128)(2,1)S(1)} %unit_keep.3.keep_ref, bf16[144,2048]{1,0:T(8,128)(2,1)S(1)} %collective-permute-done.7.got_ref), custom_call_target="tpu_custom_call" | custom-call | tf_op jit(solution)/shard_map/pack/pallas_call | solution.py:475
  6.0 33.4 %all_to_all.61.x_ref = bf16[64,24,512]{2,1,0:T(8,128)(2,1)S(1)} all-to-all(bf16[64,24,512]{2,1,0:T(8,128)(2,1)S(1)} %get-tuple-element.155), channel_id=1, replica_groups=mesh['x'=4,'z'=4,'y'=4,'c'=2] {'x','z','y'}, dimensions={0} | all-to-all | bytes 3145728 | tf_op jit(solution)/shard_map/all_to_all | solution.py:480
  39.4 1.5 %names.3 = (bf16[64,512]{1,0:T(8,128)(2,1)S(1)}, s32[8,1536]{1,0:T(8,128)S(1)}, s32[64,128]{1,0:T(8,128)S(1)}, s32[64,128]{1,0:T(8,128)S(1)}, s32[8,128]{1,0:T(8,128)S(1)}) custom-call(bf16[64,24,512]{2,1,0:T(8,128)(2,1)S(1)} %all_to_all.61.x_ref), custom_call_target="tpu_custom_call" | custom-call | tf_op jit(solution)/shard_map/names/pallas_call | solution.py:482
  40.9 0.1 collective-permute-start.8
  41.0 3.1 %sort.3 = (bf16[1216,512]{1,0:T(8,128)(2,1)S(1)}, bf16[1216,512]{1,0:T(8,128)(2,1)S(1)}) custom-call(bf16[64,24,512]{2,1,0:T(8,128)(2,1)S(1)} %all_to_all.61.x_ref, s32[8,1536]{1,0:T(8,128)S(1)} %get-tuple-element.158.line_ref), custom_call_target="tpu_custom_call" | custom-call | tf_op jit(solution)/shard_map/sort/pallas_call | solution.py:489
  44.1 0.0 collective-permute-done.8.guest_ref
  44.2 3.8 %collective-permute-start.9 = (bf16[1216,512]{1,0:T(8,128)(2,1)S(1)}, bf16[1216,512]{1,0:T(8,128)(2,1)S(1)}, u32[]{:S(2)}, u32[]{:S(2)}) collective-permute-start(bf16[1216,512]{1,0:T(8,128)(2,1)S(1)} %get-tuple-element.161), channel_id=1, source_target_pairs={{0,1},{1,0},{2,3},{3,2},{4,5},{5,4},{6,7},{7,6},{8,9},{9,8},{10,11... | collective-permute-start | bytes 3735560 | tf_op jit(solution)/shard_map/ppermute | solution.py:494
  48.0 0.0 collective-permute-start.10
  48.0 1.6 %own.3 = (f32[2496,128]{1,0:T(8,128)S(1)}, s32[8,64]{1,0:T(8,128)S(1)}) custom-call(bf16[1216,512]{1,0:T(8,128)(2,1)S(1)} %get-tuple-element.163.x_ref, bf16[64,512]{1,0:T(8,128)(2,1)S(1)} %collective-permute-done.8.guest_ref, s32[64,128]{1,0:T(8,128)S(1)} %get-tuple-element.164.key_ref, s32[64,128]{1,0:T(8,128)S(1)} %get-tuple-element.165.pos_ref), custom_call_target="tpu_custom_call" | custom-call | flops 327155712 | bytes 4194304 | tf_op jit(solution)/shard_map/own/pallas_call | solution.py:496
  49.5 1.1 %collective-permute-done.10.guest_ref = bf16[64,512]{1,0:T(8,128)(2,1)S(1)} collective-permute-done((bf16[64,512]{1,0:T(8,128)(2,1)S(1)}, bf16[64,512]{1,0:T(8,128)(2,1)S(1)}, u32[]{:S(2)}, u32[]{:S(2)}) %collective-permute-start.10) | collective-permute-done | bytes 65568 | tf_op jit(solution)/shard_map/ppermute | solution.py:495
  50.6 0.0 collective-permute-done.9.x_ref
  50.6 1.6 %gram.3 = (f32[352,128]{1,0:T(8,128)S(1)}, f32[352,128]{1,0:T(8,128)S(1)}, f32[352,128]{1,0:T(8,128)S(1)}, f32[352,128]{1,0:T(8,128)S(1)}) custom-call(s32[8,128]{1,0:T(8,128)S(1)} %get-tuple-element.156.meta_ref, bf16[1216,512]{1,0:T(8,128)(2,1)S(1)} %collective-permute-done.9.x_ref, bf16[64,512]{1,0:T(8,128)(2,1)S(1)} %collective-permute-done.10.guest_ref, ...), custom_call_target="tpu_custom_call" | custom-call | tf_op jit(solution)/shard_map/gram/pallas_call | solution.py:503
  52.2 1.2 %collective-permute-start.11 = (f32[352,128]{1,0:T(8,128)S(1)}, f32[352,128]{1,0:T(8,128)S(1)}, u32[]{:S(2)}, u32[]{:S(2)}) collective-permute-start(f32[352,128]{1,0:T(8,128)S(1)} %get-tuple-element.169), channel_id=1, source_target_pairs={{0,4},{2,6},{4,0},{6,2},{1,5},{3,7},{5,1},{7,3},{8,12},{10,14},{12... | collective-permute-start | bytes 540680 | tf_op jit(solution)/shard_map/ppermute | solution.py:511
  53.4 0.2 collective-permute-start.12
  53.6 2.4 %collective-permute-start.13 = (f32[352,128]{1,0:T(8,128)S(1)}, f32[352,128]{1,0:T(8,128)S(1)}, u32[]{:S(2)}, u32[]{:S(2)}) collective-permute-start(f32[352,128]{1,0:T(8,128)S(1)} %get-tuple-element.171), channel_id=1, source_target_pairs={{0,6},{2,0},{4,2},{6,4},{1,7},{3,1},{5,3},{7,5},{8,14},{10,8},{12,... | collective-permute-start | bytes 540680 | tf_op jit(solution)/shard_map/ppermute | solution.py:511
  56.1 0.6 fit.3
  56.6 0.5 slice.6
  57.8 2.0 %collective-permute-done.11.p1 = f32[352,128]{1,0:T(8,128)S(1)} collective-permute-done((f32[352,128]{1,0:T(8,128)S(1)}, f32[352,128]{1,0:T(8,128)S(1)}, u32[]{:S(2)}, u32[]{:S(2)}) %collective-permute-start.11) | collective-permute-done | bytes 180256 | tf_op jit(solution)/shard_map/ppermute | solution.py:511
  59.9 4.3 %collective-permute-done.12.p2 = f32[352,128]{1,0:T(8,128)S(1)} collective-permute-done((f32[352,128]{1,0:T(8,128)S(1)}, f32[352,128]{1,0:T(8,128)S(1)}, u32[]{:S(2)}, u32[]{:S(2)}) %collective-permute-start.12) | collective-permute-done | bytes 180256 | tf_op jit(solution)/shard_map/ppermute | solution.py:511
  64.2 0.0 collective-permute-done.13.p3
  64.2 1.5 %maxima.3 = f32[128,128]{1,0:T(8,128)} custom-call(s32[44,128]{1,0:T(8,128)S(1)} %get-tuple-element.174.table_ref, f32[352,128]{1,0:T(8,128)S(1)} %get-tuple-element.175.p0, f32[352,128]{1,0:T(8,128)S(1)} %collective-permute-done.11.p1, f32[352,128]{1,0:T(8,128)S(1)} %collective-permute-done.12.p2, f32[352,128]{1,0:T(8,128)S(1)} %collective-permute-done.13.p3, ...), custom_call_target="tpu_custom_call" | custom-call | tf_op jit(solution)/shard_map/maxima/pallas_call | solution.py:519
  65.6 5.1 %all-to-all-start.8 = ((f32[128,1,128]{2,1,0:T(1,128)}), f32[128,1,128]{2,1,0:T(1,128)S(1)}, u32[]{:S(2)}, u32[]{:S(2)}) async-start(f32[128,1,128]{2,1,0:T(1,128)} %bitcast.17), calls=%async_computation.8 | async-start | bytes 131072 | tf_op jit(solution)/shard_map/all_to_all | solution.py:524
  70.7 9.5 %all-to-all-done.8 = f32[128,1,128]{2,1,0:T(1,128)S(1)} async-done(((f32[128,1,128]{2,1,0:T(1,128)}), f32[128,1,128]{2,1,0:T(1,128)S(1)}, u32[]{:S(2)}, u32[]{:S(2)}) %all-to-all-start.8) | async-done | bytes 65568 | tf_op jit(solution)/shard_map/all_to_all | solution.py:524
  80.2 0.6 pick.3
  (1 shorter events, 0.0 us)
Async XLA Ops:
  0.0 3.5 %copy-start.1 = (f32[128,4096]{1,0:T(8,128)S(1)}, f32[128,4096]{1,0:T(8,128)}, u32[]{:S(2)}) copy-start(f32[128,4096]{1,0:T(8,128)} %x_ref.3) | copy-start | bytes 6291460
  0.0 3.5 %copy-start = (s32[128]{0:T(128)S(1)}, s32[128]{0:T(128)}, u32[]{:S(2)}) copy-start(s32[128]{0:T(128)} %param.9) | copy-start | bytes 1540
  2.0 3.1 %collective-permute-start.7 = (bf16[144,2048]{1,0:T(8,128)(2,1)S(1)}, bf16[144,2048]{1,0:T(8,128)(2,1)S(1)}, u32[]{:S(2)}, u32[]{:S(2)}) collective-permute-start(bf16[144,2048]{1,0:T(8,128)(2,1)S(1)} %get-tuple-element.154), channel_id=1, source_target_pairs={{0,1},{1,0},{2,3},{3,2},{4,5},{5,4},{6,7},{7,6},{8,9},{9,8},{10,11... | collective-permute-start | bytes 1769480 | tf_op jit(solution)/shard_map/ppermute | solution.py:468
  40.9 3.2 %collective-permute-start.8 = (bf16[64,512]{1,0:T(8,128)(2,1)S(1)}, bf16[64,512]{1,0:T(8,128)(2,1)S(1)}, u32[]{:S(2)}, u32[]{:S(2)}) collective-permute-start(bf16[64,512]{1,0:T(8,128)(2,1)S(1)} %get-tuple-element.157), channel_id=1, source_target_pairs={{0,24},{8,0},{16,8},{24,16},{1,25},{9,1},{17,9},{25,17},{2,26},{10... | collective-permute-start | bytes 196616 | tf_op jit(solution)/shard_map/ppermute | solution.py:487
  44.2 6.5 %collective-permute-start.9 = (bf16[1216,512]{1,0:T(8,128)(2,1)S(1)}, bf16[1216,512]{1,0:T(8,128)(2,1)S(1)}, u32[]{:S(2)}, u32[]{:S(2)}) collective-permute-start(bf16[1216,512]{1,0:T(8,128)(2,1)S(1)} %get-tuple-element.161), channel_id=1, source_target_pairs={{0,1},{1,0},{2,3},{3,2},{4,5},{5,4},{6,7},{7,6},{8,9},{9,8},{10,11... | collective-permute-start | bytes 3735560 | tf_op jit(solution)/shard_map/ppermute | solution.py:494
  48.0 2.7 %collective-permute-start.10 = (bf16[64,512]{1,0:T(8,128)(2,1)S(1)}, bf16[64,512]{1,0:T(8,128)(2,1)S(1)}, u32[]{:S(2)}, u32[]{:S(2)}) collective-permute-start(bf16[64,512]{1,0:T(8,128)(2,1)S(1)} %collective-permute-done.8.guest_ref), channel_id=1, source_target_pairs={{0,1},{1,0},{2,3},{3,2},{4,5},{5,4},{6,7},{7,6},{8,9},{9,8},{10,11... | collective-permute-start | bytes 196616 | tf_op jit(solution)/shard_map/ppermute | solution.py:495
  52.2 7.6 %collective-permute-start.11 = (f32[352,128]{1,0:T(8,128)S(1)}, f32[352,128]{1,0:T(8,128)S(1)}, u32[]{:S(2)}, u32[]{:S(2)}) collective-permute-start(f32[352,128]{1,0:T(8,128)S(1)} %get-tuple-element.169), channel_id=1, source_target_pairs={{0,4},{2,6},{4,0},{6,2},{1,5},{3,7},{5,1},{7,3},{8,12},{10,14},{12... | collective-permute-start | bytes 540680 | tf_op jit(solution)/shard_map/ppermute | solution.py:511
  53.4 10.8 %collective-permute-start.12 = (f32[352,128]{1,0:T(8,128)S(1)}, f32[352,128]{1,0:T(8,128)S(1)}, u32[]{:S(2)}, u32[]{:S(2)}) collective-permute-start(f32[352,128]{1,0:T(8,128)S(1)} %get-tuple-element.170), channel_id=1, source_target_pairs={{0,2},{2,4},{4,6},{6,0},{1,3},{3,5},{5,7},{7,1},{8,10},{10,12},{12... | collective-permute-start | bytes 540680 | tf_op jit(solution)/shard_map/ppermute | solution.py:511
  53.6 10.5 %collective-permute-start.13 = (f32[352,128]{1,0:T(8,128)S(1)}, f32[352,128]{1,0:T(8,128)S(1)}, u32[]{:S(2)}, u32[]{:S(2)}) collective-permute-start(f32[352,128]{1,0:T(8,128)S(1)} %get-tuple-element.171), channel_id=1, source_target_pairs={{0,6},{2,0},{4,2},{6,4},{1,7},{3,1},{5,3},{7,5},{8,14},{10,8},{12,... | collective-permute-start | bytes 540680 | tf_op jit(solution)/shard_map/ppermute | solution.py:511
  65.6 14.6 %all-to-all-start.8 = ((f32[128,1,128]{2,1,0:T(1,128)}), f32[128,1,128]{2,1,0:T(1,128)S(1)}, u32[]{:S(2)}, u32[]{:S(2)}) async-start(f32[128,1,128]{2,1,0:T(1,128)} %bitcast.17), calls=%async_computation.8 | async-start | bytes 131072 | tf_op jit(solution)/shard_map/all_to_all | solution.py:524
